TPU v7x, 32 devices: a whole 2x2x4 slice. The times are simulated.
32 devices in a mesh: wave: 8 (over z, y), lev: 4 (over x, core).
Axes of the slice: x: 2, y: 2, z: 4, core: 2. Of those that a mesh axis runs over, the one named last changes fastest.
Arguments:
- control: bfloat16 [32, 1281, 512], P(('wave', 'lev')), may hold values from -6 to 6
- covariance: float32 [1280, 128, 128], P(('wave', 'lev')), may hold values from -0.5 to 0.5
- legendre: bfloat16 [32, 1281, 2560], P(('wave', 'lev')), may hold values from -0.25 to 0.25
- pair_order: int32 [32], P(('wave', 'lev')), may hold values from 0 to 639, as said below
- band_rows: int32 [8], replicated, may hold values from 1 to 400, 2560 in all
Outputs:
- fourier: bfloat16 [64, 3200, 512], P(None, 'wave', 'lev')
Inputs may be any that keep to these rules, and one draw needn't show every extreme that they name: `pair_order`: the pair holds zonal wavenumbers m and 1279 - m; values may repeat. `band_rows`: band sizes sum to 2560; bands follow one another from latitude 0.
All inputs are finite; a program needn't handle non-finite values.
Results may differ from a plain program's by a relative error of at most 0.0049.
Values may be sent and summed in bfloat16 or wider, within the bound.
No kernel may reach another device: no remote copies, remote signals or barrier semaphores. Data moves between devices by JAX's collectives and lax.ppermute only.
A program may use at most 128 MiB of HBM per device.

v0:
```python
import functools

import jax
import jax.numpy as jnp
import numpy as np
from jax import lax
from jax.experimental import pallas as pl
from jax.experimental.pallas import tpu as pltpu
from jax.sharding import PartitionSpec as P

BF = jnp.bfloat16
F32 = jnp.float32
SUB = 16
DIGIT = 16


def ceil_to(value, step):
    return (value + step - 1) // step * step


class Plan:
    def __init__(self, devices, degrees):
        self.devices = devices
        self.group = devices // 2
        self.degrees = degrees
        self.block = degrees // devices
        self.chunks = []
        row, fold = 0, 0
        for count in self.fold_counts(self.block):
            self.chunks.append((row, fold, count))
            row += ceil_to(2 * count, SUB)
            fold += count
        self.rows = row
        whole = [(at, n) for at, (_, _, n) in enumerate(self.chunks) if n % SUB == 0]
        mixed = [(at, n) for at, (_, _, n) in enumerate(self.chunks) if n % SUB]
        lower = [(at, 0, n) for at, n in whole] + [(at, 0, ceil_to(2 * n, SUB)) for at, n in mixed]
        self.segments = lower + [(at, n, n) for at, n in whole]
        self.widths = [
            self.group * sum(n for _, _, n in self.segments),
            self.group * sum(n for _, _, n in lower),
        ]

    @staticmethod
    def fold_counts(block):
        return (block - 8, 8) if block % SUB == 8 and block > 8 else (block,)

    def chunk_rows(self, at):
        _, first, count = self.chunks[at]
        height = ceil_to(2 * count, SUB)
        fold = np.zeros(height, np.int32)
        fold[:2 * count] = first + np.tile(np.arange(count), 2)
        row = np.arange(height)
        return fold, row < count, row < 2 * count

    def message_rows(self):
        tables = [self.chunk_rows(at) for at in range(len(self.chunks))]
        one = [np.concatenate(column) for column in zip(*tables)]
        return [np.repeat(np.arange(self.group, dtype=np.int32), self.rows)] + [
            np.tile(column, self.group) for column in one
        ]

    def transform_rows(self):
        parts = []
        for at, first, count in self.segments:
            columns = [column[first:first + count] for column in self.chunk_rows(at)]
            parts.append(
                [np.repeat(np.arange(self.group, dtype=np.int32), count)]
                + [np.tile(column, self.group) for column in columns]
            )
        return [np.concatenate(column) for column in zip(*parts)]

    def extra_row(self, message, fold):
        base, result = 0, jnp.int32(0)
        for at, first, count in self.segments:
            if first == 0:
                start = self.chunks[at][1]
                here = (fold >= start) & (fold < start + self.chunks[at][2])
                result = jnp.where(here, base + message * count + fold - start, result)
            base += self.group * count
        return result


def pack_kernel(plan, levels, info_ref, slot_ref, control_ref, out_ref):
    slots = control_ref.shape[0]
    messages = out_ref.shape[0]
    even = slots - 1
    rows = messages * plan.rows
    slot = slot_ref[...]
    pick = (slot == lax.broadcasted_iota(jnp.int32, (rows, even), 1)).astype(F32).astype(BF)
    got = jnp.dot(pick, control_ref[:even, :], preferred_element_type=F32)
    last = control_ref[even:slots, :].astype(F32)
    got = jnp.where(slot == even, last, got).astype(BF)
    extra_slot = plan.degrees - info_ref[0]
    lane = lax.broadcasted_iota(jnp.int32, (SUB, even), 1)
    first = lax.broadcasted_iota(jnp.int32, (SUB, even), 0) == 0
    choose = jnp.where(first & (lane == extra_slot), 1.0, 0.0).astype(BF)
    extra = jnp.dot(choose, control_ref[:even, :], preferred_element_type=F32)
    extra = jnp.where(extra_slot == even, last, extra)
    place = lax.broadcasted_iota(jnp.int32, (SUB, levels), 0)
    tail = jnp.zeros((SUB, levels), F32)
    for c in range(4):
        tail = jnp.where(place == c, extra[0:1, c * levels:(c + 1) * levels], tail)
    high_digit = (info_ref[0] // DIGIT).astype(F32)
    low_digit = (info_ref[0] % DIGIT).astype(F32)
    tail = jnp.where(place == 4, high_digit, jnp.where(place == 5, low_digit, tail)).astype(BF)
    for k in range(messages):
        for c in range(4):
            out_ref[k, c * plan.rows:(c + 1) * plan.rows, :] = got[
                k * plan.rows:(k + 1) * plan.rows, c * levels:(c + 1) * levels
            ]
        out_ref[k, 4 * plan.rows:, :] = tail


def pack(plan, control, lowest, slots_of_rows):
    slots, columns = control.shape
    levels = columns // 4
    height = 4 * plan.rows + SUB
    per_step = max(1, min(plan.group, 320 // plan.rows))
    return pl.pallas_call(
        functools.partial(pack_kernel, plan, levels),
        grid=(plan.group // per_step,),
        out_shape=jax.ShapeDtypeStruct((plan.group, height, levels), BF),
        in_specs=[
            pl.BlockSpec(memory_space=pltpu.SMEM),
            pl.BlockSpec((per_step * plan.rows, 1), lambda k: (k, 0)),
            pl.BlockSpec((slots, columns), lambda k: (0, 0)),
        ],
        out_specs=pl.BlockSpec((per_step, height, levels), lambda k: (k, 0, 0)),
        compiler_params=pltpu.CompilerParams(vmem_limit_bytes=16 * 1024 * 1024),
        cost_estimate=pl.CostEstimate(flops=1, bytes_accessed=1, transcendentals=0),
        name="pack_rows",
    )(lowest, slots_of_rows, control)


def table_kernel(plan, upper_ref, lower_ref, legendre_ref, *refs):
    outs, picks = refs[:2], refs[2:]
    slots = legendre_ref.shape[0]
    even = slots - 1

    @pl.when(pl.program_id(0) == 0)
    def _():
        for index_ref, pick_ref in zip((upper_ref, lower_ref), picks):
            slot = lax.broadcasted_iota(jnp.int32, pick_ref.shape, 0)
            pick_ref[...] = jnp.where(slot == index_ref[...], 1.0, 0.0).astype(BF)

    def times(rows, picked):
        return lax.dot_general(rows, picked, (((0,), (0,)), ((), ())), preferred_element_type=F32)

    for out_ref, pick_ref in zip(outs, picks):
        got = times(legendre_ref[:even, :], pick_ref[:even, :])
        last = jnp.concatenate(
            [legendre_ref[even:slots, :].astype(F32), jnp.zeros((SUB - 1, legendre_ref.shape[1]), F32)], axis=0
        ).astype(BF)
        out_ref[...] = (got + times(last, pick_ref[even:even + SUB, :])).astype(BF)


def make_tables(plan, legendre, slots_of_rows):
    slots, latitudes = legendre.shape
    tile = 256
    index = [rows[None, :width] for rows, width in zip(slots_of_rows, plan.widths)]
    return pl.pallas_call(
        functools.partial(table_kernel, plan),
        grid=(latitudes // tile,),
        out_shape=[jax.ShapeDtypeStruct((latitudes, width), BF) for width in plan.widths],
        in_specs=[pl.BlockSpec((1, width), lambda t: (0, 0)) for width in plan.widths]
        + [pl.BlockSpec((slots, tile), lambda t: (0, t))],
        out_specs=[pl.BlockSpec((tile, width), lambda t: (t, 0)) for width in plan.widths],
        scratch_shapes=[pltpu.VMEM((slots - 1 + SUB, width), BF) for width in plan.widths],
        compiler_params=pltpu.CompilerParams(vmem_limit_bytes=20 * 1024 * 1024),
        cost_estimate=pl.CostEstimate(
            flops=20 * latitudes * slots * sum(plan.widths), bytes_accessed=2 * legendre.size, transcendentals=0
        ),
        name="make_tables",
    )(*index, legendre)


def swap_matrix():
    i = lax.broadcasted_iota(jnp.int32, (SUB * SUB, SUB * SUB), 0)
    j = lax.broadcasted_iota(jnp.int32, (SUB * SUB, SUB * SUB), 1)
    return jnp.where((i // SUB == j % SUB) & (i % SUB == j // SUB), 1.0, 0.0).astype(BF)


def filter_kernel(plan, levels, info_ref, rows_ref, *refs):
    *blocks, out_ref, held_ref, x_ref, y_ref, z_ref, in_sems, out_sems = refs
    pieces = len(blocks) // 2
    each = plan.block // pieces
    first_fold = info_ref[1].astype(F32)
    swap = swap_matrix()

    arrivals = []
    for at, block in enumerate(blocks):
        place = info_ref[0] if at < pieces else 1 - info_ref[0]
        folds = pl.ds(at % pieces * each, each)
        arrivals.append(pltpu.make_async_copy(block, held_ref.at[place, folds], in_sems.at[at]))
        arrivals[at].start()

    def low_matrix(fold):
        return held_ref[0, fold]

    def high_matrix(fold):
        return held_ref[1, fold // each * each + each - 1 - fold % each]

    def times(rows, matrix):
        return lax.dot_general(rows, matrix, (((1,), (1,)), ((), ())), preferred_element_type=F32)

    def turn(rows):
        return jnp.dot(swap, rows, preferred_element_type=F32)

    groups = plan.group // SUB
    held = plan.rows * SUB
    for g in range(groups):
        sources = slice(g * SUB, (g + 1) * SUB)
        for r in range(0, plan.rows, SUB):
            parts = []
            for c in range(4):
                start = c * plan.rows + r
                parts.append(rows_ref[sources, start:start + SUB, :].reshape(SUB * SUB, levels))
            x_ref[g * held + r * SUB:g * held + (r + SUB) * SUB, :] = turn(jnp.concatenate(parts, axis=1)).astype(BF)

    for arrival in arrivals:
        arrival.wait()

    departures = []

    def send(rows):
        at = len(departures)
        departures.append(pltpu.make_async_copy(z_ref.at[:, rows, :], out_ref.at[:, rows, :], out_sems.at[at]))
        departures[at].start()

    tails = []
    for g in range(groups):
        sources = slice(g * SUB, (g + 1) * SUB)
        tail = turn(rows_ref[sources, 4 * plan.rows:4 * plan.rows + SUB, :].reshape(SUB * SUB, levels))
        low = tail[4 * SUB:5 * SUB] * DIGIT + tail[5 * SUB:6 * SUB]
        tails.append([tail[:4 * SUB].astype(BF), jnp.concatenate([low] * 4, axis=0), jnp.zeros((4 * SUB, levels), F32)])

    for row0, fold0, count in plan.chunks:
        height = ceil_to(2 * count, SUB)
        for g in range(groups):
            sources = slice(g * SUB, (g + 1) * SUB)
            extra, low, kept = tails[g]
            for i in range(count):
                def stack(row):
                    at = g * held + row * SUB
                    return jnp.concatenate(
                        [x_ref[at:at + SUB, c * levels:(c + 1) * levels] for c in range(4)], axis=0
                    )

                folded, high = stack(row0 + i), stack(row0 + count + i)
                from_low = times(folded, low_matrix(fold0 + i))
                from_high = times(jnp.concatenate([folded, high, extra], axis=0), high_matrix(fold0 + i))
                fold = first_fold + (fold0 + i)
                mixed = jnp.where(low <= fold, from_low, from_high[:4 * SUB])
                kept = jnp.where(low == fold, from_high[8 * SUB:], kept)
                for row, value in ((row0 + i, mixed), (row0 + count + i, from_high[4 * SUB:8 * SUB])):
                    value = value.astype(BF)
                    for c in range(4):
                        y_ref[row * SUB:(row + 1) * SUB, c * levels:(c + 1) * levels] = value[c * SUB:(c + 1) * SUB]
            tails[g][2] = kept
            if height > 2 * count:
                y_ref[(row0 + 2 * count) * SUB:(row0 + height) * SUB, :] = jnp.zeros(
                    ((height - 2 * count) * SUB, 4 * levels), BF
                )
            for r in range(row0, row0 + height, SUB):
                back = turn(y_ref[r * SUB:(r + SUB) * SUB, :]).astype(BF)
                for c in range(4):
                    start = c * plan.rows + r
                    z_ref[sources, start:start + SUB, :] = back[:, c * levels:(c + 1) * levels].reshape(
                        SUB, SUB, levels
                    )
        for c in range(4):
            send(pl.ds(c * plan.rows + row0, height))
    for g in range(groups):
        sources = slice(g * SUB, (g + 1) * SUB)
        filled = jnp.concatenate([tails[g][2], jnp.zeros((12 * SUB, levels), F32)], axis=0).astype(BF)
        z_ref[sources, 4 * plan.rows:4 * plan.rows + SUB, :] = turn(filled).astype(BF).reshape(SUB, SUB, levels)
    send(pl.ds(4 * plan.rows, SUB))
    for departure in departures:
        departure.wait()


def filter_rows(plan, info, received, near_blocks, far_blocks):
    levels = received.shape[2]
    blocks = [*near_blocks, *far_blocks]
    smem, vmem = pl.BlockSpec(memory_space=pltpu.SMEM), pl.BlockSpec(memory_space=pltpu.VMEM)
    anywhere = pl.BlockSpec(memory_space=pl.ANY)
    return pl.pallas_call(
        functools.partial(filter_kernel, plan, levels),
        out_shape=jax.ShapeDtypeStruct(received.shape, BF),
        in_specs=[smem, vmem] + [anywhere] * len(blocks),
        out_specs=anywhere,
        scratch_shapes=[
            pltpu.VMEM((2, plan.block, levels, levels), BF),
            pltpu.VMEM((plan.group * plan.rows, 4 * levels), BF),
            pltpu.VMEM((plan.rows * SUB, 4 * levels), BF),
            pltpu.VMEM(received.shape, BF),
            pltpu.SemaphoreType.DMA((len(blocks),)),
            pltpu.SemaphoreType.DMA((4 * len(plan.chunks) + 1,)),
        ],
        compiler_params=pltpu.CompilerParams(vmem_limit_bytes=20 * 1024 * 1024),
        cost_estimate=pl.CostEstimate(
            flops=2 * plan.group * 16 * plan.block * levels * levels * 4,
            bytes_accessed=2 * 2 * received.size + 4 * plan.block * levels * levels,
            transcendentals=0,
        ),
        name="filter_rows",
    )(info, received, *blocks)


def grid_kernel(plan, levels, latitudes, depth, level_cols, tile, info_ref, starts_ref, bands_ref, part_ref, *refs):
    tables, out_ref, held_tables = refs[:2], refs[2], refs[3:5]
    upper_ref, lower_ref, *grids, cut_ref, sems, out_sems = refs[5:]
    waves = bands_ref.shape[0]
    groups = 4 * levels // level_cols
    tiles = [slice(start, stop) for start, stop in zip(tile, tile[1:])]

    def copy(half, at):
        rows = tiles[at]
        return pltpu.make_async_copy(tables[half].at[rows], held_tables[half].at[rows], sems.at[half, at])

    for half in (1, 0):
        for at in range(len(tiles)):
            copy(half, at).start()

    base = 0
    for at, first, rows in plan.segments:
        for k in range(plan.group):
            for c in range(4):
                start = c * plan.rows + plan.chunks[at][0] + first
                cols = slice(c * levels, (c + 1) * levels)
                value = part_ref[k, start:start + rows, :]
                upper_ref[base + k * rows:base + (k + 1) * rows, cols] = value
                if base < plan.widths[1]:
                    lower_ref[base + k * rows:base + (k + 1) * rows, cols] = value
        base += plan.group * rows

    extra = part_ref[info_ref[0], 4 * plan.rows:4 * plan.rows + SUB, :]
    base = info_ref[1] // SUB * SUB
    place = pl.ds(pl.multiple_of(base, SUB), SUB)
    here = lax.broadcasted_iota(jnp.int32, (SUB, levels), 0) == info_ref[1] - base
    for c in range(4):
        cols = slice(c * levels, (c + 1) * levels)
        held = upper_ref[place, cols].astype(F32)
        lower_ref[place, cols] = jnp.where(here, extra[c:c + 1, :].astype(F32), held).astype(BF)

    def transform(half, at):
        copy(half, at).wait()
        rows = tiles[at]
        grids[half][rows, :] = jnp.dot(
            held_tables[half][rows, :], (upper_ref, lower_ref)[half][...], preferred_element_type=F32
        )

    def departure(half, w):
        messages = pl.ds(w * groups, groups)
        return pltpu.make_async_copy(cut_ref.at[messages, half], out_ref.at[messages, half], out_sems.at[half, w])

    def cut(half, w):
        place = lax.broadcasted_iota(jnp.int32, (8, 4 * levels), 0)
        start = starts_ref[w]
        base = start // 8 * 8
        offset = start - base

        def slab(at):
            held = grids[half][pl.ds(pl.multiple_of(base + at, 8), 8), :]
            return pltpu.roll(held, (8 - offset) % 8, axis=0)

        after = slab(0)
        done = []
        for r in range(0, depth, 8):
            now, after = after, slab(r + 8)
            got = jnp.where(place < 8 - offset, now, after)
            done.append(jnp.where(place < bands_ref[w] - r, got, 0.0))
            if len(done) == 2 or r + 8 == depth:
                rows = jnp.concatenate(done, axis=0).astype(BF)
                first = r + 8 - rows.shape[0]
                for g in range(groups):
                    cut_ref[w * groups + g, half, first:r + 8, :] = rows[:, g * level_cols:(g + 1) * level_cols]
                done = []
        departure(half, w).start()

    for at in range(len(tiles)):
        transform(1, at)
    for at in range(len(tiles)):
        transform(0, at)
        for w in range(at * waves // len(tiles), (at + 1) * waves // len(tiles)):
            cut(1, w)
    for w in range(waves):
        cut(0, w)
    for half in range(2):
        for w in range(waves):
            departure(half, w).wait()


def to_bands(plan, info, starts, bands, part, tables, depth, level_cols):
    latitudes = tables[0].shape[0]
    levels = part.shape[2]
    columns = 4 * levels
    tile = [0] + list(range(latitudes // 5, latitudes + 1, 2 * latitudes // 5))
    smem, vmem = pl.BlockSpec(memory_space=pltpu.SMEM), pl.BlockSpec(memory_space=pltpu.VMEM)
    messages = bands.shape[0] * columns // level_cols
    grid = pltpu.VMEM((ceil_to(latitudes + depth, 8) + 8, columns), F32)
    held = 2 * (latitudes + columns) * sum(plan.widths) + 8 * (latitudes + depth) * columns
    held += 4 * messages * depth * ceil_to(level_cols, 128) + 2 * part.size
    limit = max(52 * 1024 * 1024, held + 4 * 1024 * 1024)
    return pl.pallas_call(
        functools.partial(grid_kernel, plan, levels, latitudes, depth, level_cols, tile),
        out_shape=jax.ShapeDtypeStruct((messages, 2, depth, level_cols), BF),
        in_specs=[smem, smem, smem, vmem] + [pl.BlockSpec(memory_space=pl.ANY)] * 2,
        out_specs=pl.BlockSpec(memory_space=pl.ANY),
        scratch_shapes=[
            pltpu.VMEM(tables[0].shape, BF),
            pltpu.VMEM(tables[1].shape, BF),
            pltpu.VMEM((plan.widths[0], columns), BF),
            pltpu.VMEM((plan.widths[1], columns), BF),
            grid,
            grid,
            pltpu.VMEM((messages, 2, depth, level_cols), BF),
            pltpu.SemaphoreType.DMA((2, len(tile) - 1)),
            pltpu.SemaphoreType.DMA((2, bands.shape[0])),
        ],
        compiler_params=pltpu.CompilerParams(vmem_limit_bytes=limit),
        cost_estimate=pl.CostEstimate(
            flops=2 * latitudes * sum(plan.widths) * columns,
            bytes_accessed=2 * latitudes * sum(plan.widths) + 4 * messages * depth * level_cols,
            transcendentals=0,
        ),
        name="grid_bands",
    )(info, starts, bands, part, *tables)


def per_device(control, covariance, legendre, pair_order, band_rows):
    axes = ("wave", "lev")
    waves, lev_count = lax.axis_size("wave"), lax.axis_size("lev")
    _, slots, columns = control.shape
    degrees, levels = slots - 1, columns // 4
    latitudes = legendre.shape[2]
    depth = 5 * latitudes // (4 * waves)
    level_cols = columns // lev_count
    plan = Plan(waves * lev_count, degrees)
    group, block = plan.group, plan.block
    me = lax.axis_index("wave") * lev_count + lax.axis_index("lev")
    is_high = (me >= group).astype(jnp.int32)
    lowest = pair_order[0]
    halves = [list(range(group)), list(range(group, 2 * group))]

    def exchange(rows):
        return lax.all_to_all(rows, axes, split_axis=0, concat_axis=0, tiled=True, axis_index_groups=halves)

    plane = group // 2
    whole = range(2 * group)
    far = [(d, (3 - d // plane) * plane + d % plane) for d in whole]
    near = [(d, d // plane * plane + plane - 1 - d % plane) for d in whole]
    pieces = 2 if block % 2 == 0 else 1
    each = block // pieces
    own = []
    for fold in range(0, block, each):
        start = jnp.where(is_high == 1, block - fold - each, fold)
        own.append(lax.dynamic_slice_in_dim(covariance, start, each, 0).astype(BF))
        own[-1], covariance = lax.optimization_barrier((own[-1], covariance))
    *own, control = lax.optimization_barrier((*own, control))
    far_blocks = [lax.ppermute(part, axes, far) for part in own]
    near_blocks = [lax.ppermute(part, axes, near) for part in own]

    def fold_block(rank):
        rank = jnp.where(is_high == 1, group - 1 - rank, rank)
        return rank // plane * plane + plane - 1 - rank % plane

    def slots_of(message, fold, folded, used):
        degree = fold_block(message) * block + fold
        upper = jnp.where(folded, degree - lowest, degrees - 1 - degree - lowest)
        upper = jnp.where(used & (upper >= 0), upper, -1)
        lower = jnp.where(used & folded & (degree <= lowest), degrees - degree, -1)
        return upper, lower

    upper, lower = slots_of(*plan.message_rows())
    sent = jnp.where(upper >= 0, upper, lower)
    received = exchange(pack(plan, control[0], pair_order, sent[:, None]))

    tables = make_tables(plan, legendre[0], slots_of(*plan.transform_rows()))

    info = jnp.stack([is_high, fold_block(me - group * is_high) * block])
    received, tables = lax.optimization_barrier((received, tables))
    filtered = exchange(filter_rows(plan, info, received, near_blocks, far_blocks))

    extra_block = lowest // block
    extra_message = fold_block(extra_block)
    extra_row = plan.extra_row(extra_message, lowest - extra_block * block)
    where = jnp.stack([extra_message, extra_row])
    starts = jnp.cumsum(band_rows) - band_rows
    outgoing = to_bands(plan, where, starts, band_rows, filtered, tables, depth, level_cols)
    outgoing = outgoing.reshape(-1, depth, level_cols)
    return lax.all_to_all(outgoing, axes, split_axis=0, concat_axis=0, tiled=True)


def solution(mesh):
    return jax.shard_map(
        per_device,
        mesh=mesh,
        in_specs=(
            P(("wave", "lev"), None, None),
            P(("wave", "lev"), None, None),
            P(("wave", "lev"), None, None),
            P(("wave", "lev")),
            P(),
        ),
        out_specs=P(None, "wave", "lev"),
        check_vma=False,
    )
```

profile of v0, /device:TPU:0, one launch (start us, length us, event | category | flops | bytes accessed | tf_op | source)
XLA Modules:
  0.0 260.4 jit_solution(15500847183041362465)
XLA Ops:
  0.0 1.7 copy-done
  1.7 0.9 dynamic-slice_convert_fusion.1
  2.7 1.0 dynamic-slice_convert_fusion
  3.6 5.0 %collective-permute-start.2 = (bf16[20,128,128]{2,1,0:T(8,128)(2,1)}, bf16[20,128,128]{2,1,0:T(8,128)(2,1)S(1)}, u32[]{:S(2)}, u32[]{:S(2)}) collective-permute-start(bf16[20,128,128]{2,1,0:T(8,128)(2,1)} %dynamic-slice_convert_fusion.1), channel_id=1, source_target_pairs={{0,24},{1,25},{2,26},{3,27},{4,28},{5,29},{6,30},{7,31},{8,16},{9,... | collective-permute-start | bytes 1966088 | tf_op jit(solution)/shard_map/ppermute | solution.py:461
  8.7 1.6 collective-permute-start
  10.3 0.3 collective-permute-start.3
  10.6 0.8 collective-permute-start.1
  12.1 0.2 broadcast_in_dim.17.slot_ref
  12.4 3.2 %pack_rows.1 = bf16[16,336,128]{2,1,0:T(8,128)(2,1)S(1)} custom-call(s32[1]{0:T(128)} %copy.20.info_ref, s32[1280,1]{1,0:T(8,128)S(1)} %broadcast_in_dim.17.slot_ref, bf16[1281,512]{1,0:T(8,128)(2,1)S(1)} %bitcast.18), custom_call_target="tpu_custom_call" | custom-call | flops 1 | bytes 1 | tf_op jit(solution)/shard_map/pack_rows/pallas_call | solution.py:119
  15.6 1.1 copy-done.2
  16.7 4.4 %all-to-all-start = ((bf16[16,336,128]{2,1,0:T(8,128)(2,1)}), bf16[16,336,128]{2,1,0:T(8,128)(2,1)}, u32[]{:S(2)}, u32[]{:S(2)}) async-start(bf16[16,336,128]{2,1,0:T(8,128)(2,1)} %copy-done.2), calls=%async_computation | async-start | bytes 2752512 | tf_op jit(solution)/shard_map/all_to_all | solution.py:447
  21.2 2.9 %copy-done.4 = bf16[1,1281,2560]{2,1,0:T(8,128)(2,1)S(1)} copy-done((bf16[1,1281,2560]{2,1,0:T(8,128)(2,1)S(1)}, bf16[1,1281,2560]{2,1,0:T(8,128)(2,1)}, u32[]{:S(2)}) %copy-start.4) | copy-done | bytes 6558744
  24.1 19.7 %make_tables.1 = (bf16[2560,1280]{1,0:T(8,128)(2,1)S(1)}, bf16[2560,768]{1,0:T(8,128)(2,1)S(1)}) custom-call(s32[1,1280]{1,0:T(1,128)S(1)} %broadcast_in_dim.15.upper_ref, s32[1,768]{1,0:T(1,128)S(1)} %broadcast_in_dim.16.lower_ref, bf16[1281,2560]{1,0:T(8,128)(2,1)S(1)} %bitcast.19), custom_call_target="tpu_custom_call" | custom-call | flops 134322585600 | bytes 6558720 | tf_op jit(solution)/shard_map/make_tables/pallas_call | solution.py:161
  43.8 2.8 %copy-done.6 = bf16[2560,1280]{1,0:T(8,128)(2,1)} copy-done((bf16[2560,1280]{1,0:T(8,128)(2,1)}, bf16[2560,1280]{1,0:T(8,128)(2,1)S(1)}, u32[]{:S(2)}) %copy-start.6) | copy-done | bytes 6553624
  46.6 2.0 copy-done.7
  48.7 8.6 %all-to-all-done.rows_ref = bf16[16,336,128]{2,1,0:T(8,128)(2,1)} async-done(((bf16[16,336,128]{2,1,0:T(8,128)(2,1)}), bf16[16,336,128]{2,1,0:T(8,128)(2,1)}, u32[]{:S(2)}, u32[]{:S(2)}) %all-to-all-start) | async-done | bytes 1376288 | tf_op jit(solution)/shard_map/all_to_all | solution.py:447
  57.3 5.9 %filter_rows.1 = bf16[16,336,128]{2,1,0:T(8,128)(2,1)S(1)} custom-call(s32[2]{0:T(128)S(1)} %pad_add_fusion.1.info_ref, bf16[16,336,128]{2,1,0:T(8,128)(2,1)} %all-to-all-done.rows_ref, bf16[20,128,128]{2,1,0:T(8,128)(2,1)} %collective-permute-done.refs_0_, bf16[20,128,128]{2,1,0:T(8,128)(2,1)} %collective-permute-done.1.refs_1_, ...), custom_call_target="tpu_custom_call" | custom-call | flops 1342177280 | bytes 5373952 | tf_op jit(solution)/shard_map/filter_rows/pallas_call | solution.py:287
  63.1 1.1 copy-done.1
  64.2 11.8 %all-to-all-start.1 = ((bf16[16,336,128]{2,1,0:T(8,128)(2,1)}), bf16[16,336,128]{2,1,0:T(8,128)(2,1)}, u32[]{:S(2)}, u32[]{:S(2)}) async-start(bf16[16,336,128]{2,1,0:T(8,128)(2,1)} %copy-done.1), calls=%async_computation.1 | async-start | bytes 2752512 | tf_op jit(solution)/shard_map/all_to_all | solution.py:447
  76.1 0.2 reduce-window.9
  76.4 19.8 %all-to-all-done.1.part_ref = bf16[16,336,128]{2,1,0:T(8,128)(2,1)} async-done(((bf16[16,336,128]{2,1,0:T(8,128)(2,1)}), bf16[16,336,128]{2,1,0:T(8,128)(2,1)}, u32[]{:S(2)}, u32[]{:S(2)}) %all-to-all-start.1) | async-done | bytes 1376288 | tf_op jit(solution)/shard_map/all_to_all | solution.py:447
  96.2 11.7 %grid_bands.1 = bf16[32,2,400,128]{3,2,1,0:T(8,128)(2,1)} custom-call(s32[2]{0:T(128)S(1)} %pad_add_fusion.info_ref, s32[8]{0:T(128)S(1)} %bitcast_subtract_fusion.starts_ref, s32[8]{0:T(128)S(1)} %copy-done.5, bf16[16,336,128]{2,1,0:T(8,128)(2,1)} %all-to-all-done.1.part_ref, bf16[2560,1280]{1,0:T(8,128)(2,1)} %copy-done.6, bf16[2560,768]{1,0:T(8,128)(2,1)} %copy-done.7), custom_call_target="tpu_custom_call" | custom-call | flops 5368709120 | bytes 17039360 | tf_op jit(solution)/shard_map/grid_bands/pallas_call | solution.py:405
  107.9 149.8 %all_to_all.15 = bf16[64,400,128]{2,1,0:T(8,128)(2,1)S(1)} all-to-all(bf16[64,400,128]{2,1,0:T(8,128)(2,1)} %bitcast.21), channel_id=1, replica_groups=mesh['wave'=8,'lev'=4] {'wave','lev'}, dimensions={0} | all-to-all | bytes 13107200 | tf_op jit(solution)/shard_map/all_to_all | solution.py:492
  257.6 2.8 %copy.21 = bf16[64,400,128]{2,1,0:T(8,128)(2,1)} copy(bf16[64,400,128]{2,1,0:T(8,128)(2,1)S(1)} %all_to_all.15) | data formatting | bytes 13107200
  (38 shorter events, 0.3 us)
Async XLA Ops:
  0.0 1.7 copy-start
  0.0 12.0 %copy-start.15 = (pred[1280]{0:T(1024)(128)(4,1)S(1)}, pred[1280]{0:T(1024)(128)(4,1)}, u32[]{:S(2)}) copy-start(pred[1280]{0:T(1024)(128)(4,1)} %constant.141.clone) | copy-start | bytes 3844
  0.0 12.0 %copy-start.11 = (s32[1280]{0:T(1024)S(1)}, s32[1280]{0:T(1024)}, u32[]{:S(2)}) copy-start(s32[1280]{0:T(1024)} %constant.140.clone) | copy-start | bytes 15364
  0.0 12.0 %copy-start.12 = (s32[1280]{0:T(1024)S(1)}, s32[1280]{0:T(1024)}, u32[]{:S(2)}) copy-start(s32[1280]{0:T(1024)} %constant.139.clone) | copy-start | bytes 15364
  0.0 12.0 %copy-start.13 = (s32[1280]{0:T(1024)S(1)}, s32[1280]{0:T(1024)}, u32[]{:S(2)}) copy-start(s32[1280]{0:T(1024)} %constant.138.clone) | copy-start | bytes 15364
  1.7 10.6 %copy-start.3 = (bf16[1,1281,512]{2,1,0:T(8,128)(2,1)S(1)}, bf16[1,1281,512]{2,1,0:T(8,128)(2,1)}, u32[]{:S(2)}) copy-start(bf16[1,1281,512]{2,1,0:T(8,128)(2,1)} %param.17) | copy-start | bytes 3935236
  3.6 53.6 %collective-permute-start.2 = (bf16[20,128,128]{2,1,0:T(8,128)(2,1)}, bf16[20,128,128]{2,1,0:T(8,128)(2,1)S(1)}, u32[]{:S(2)}, u32[]{:S(2)}) collective-permute-start(bf16[20,128,128]{2,1,0:T(8,128)(2,1)} %dynamic-slice_convert_fusion.1), channel_id=1, source_target_pairs={{0,24},{1,25},{2,26},{3,27},{4,28},{5,29},{6,30},{7,31},{8,16},{9,... | collective-permute-start | bytes 1966088 | tf_op jit(solution)/shard_map/ppermute | solution.py:461
  8.7 48.5 %collective-permute-start = (bf16[20,128,128]{2,1,0:T(8,128)(2,1)}, bf16[20,128,128]{2,1,0:T(8,128)(2,1)}, u32[]{:S(2)}, u32[]{:S(2)}) collective-permute-start(bf16[20,128,128]{2,1,0:T(8,128)(2,1)} %dynamic-slice_convert_fusion.1), channel_id=1, source_target_pairs={{0,7},{1,6},{2,5},{3,4},{4,3},{5,2},{6,1},{7,0},{8,15},{9,14},{10,... | collective-permute-start | bytes 1966088 | tf_op jit(solution)/shard_map/ppermute | solution.py:462
  10.3 46.9 %collective-permute-start.3 = (bf16[20,128,128]{2,1,0:T(8,128)(2,1)}, bf16[20,128,128]{2,1,0:T(8,128)(2,1)}, u32[]{:S(2)}, u32[]{:S(2)}) collective-permute-start(bf16[20,128,128]{2,1,0:T(8,128)(2,1)} %dynamic-slice_convert_fusion), channel_id=1, source_target_pairs={{0,24},{1,25},{2,26},{3,27},{4,28},{5,29},{6,30},{7,31},{8,16},{9,... | collective-permute-start | bytes 1966088 | tf_op jit(solution)/shard_map/ppermute | solution.py:461
  10.6 46.7 %collective-permute-start.1 = (bf16[20,128,128]{2,1,0:T(8,128)(2,1)}, bf16[20,128,128]{2,1,0:T(8,128)(2,1)}, u32[]{:S(2)}, u32[]{:S(2)}) collective-permute-start(bf16[20,128,128]{2,1,0:T(8,128)(2,1)} %dynamic-slice_convert_fusion), channel_id=1, source_target_pairs={{0,7},{1,6},{2,5},{3,4},{4,3},{5,2},{6,1},{7,0},{8,15},{9,14},{10,... | collective-permute-start | bytes 1966088 | tf_op jit(solution)/shard_map/ppermute | solution.py:462
  12.3 8.8 %copy-start.8 = (s32[1280]{0:T(1024)S(1)}, s32[1280]{0:T(1024)}, u32[]{:S(2)}) copy-start(s32[1280]{0:T(1024)} %constant.145.clone) | copy-start | bytes 15364
  12.3 8.8 %copy-start.9 = (s32[1280]{0:T(1024)S(1)}, s32[1280]{0:T(1024)}, u32[]{:S(2)}) copy-start(s32[1280]{0:T(1024)} %constant.144.clone) | copy-start | bytes 15364
  12.3 8.8 %copy-start.10 = (s32[1280]{0:T(1024)S(1)}, s32[1280]{0:T(1024)}, u32[]{:S(2)}) copy-start(s32[1280]{0:T(1024)} %constant.143.clone) | copy-start | bytes 15364
  12.3 8.8 %copy-start.14 = (pred[1280]{0:T(1024)(128)(4,1)S(1)}, pred[1280]{0:T(1024)(128)(4,1)}, u32[]{:S(2)}) copy-start(pred[1280]{0:T(1024)(128)(4,1)} %constant.146.clone) | copy-start | bytes 3844
  15.6 1.1 copy-start.2
  16.7 40.5 %all-to-all-start = ((bf16[16,336,128]{2,1,0:T(8,128)(2,1)}), bf16[16,336,128]{2,1,0:T(8,128)(2,1)}, u32[]{:S(2)}, u32[]{:S(2)}) async-start(bf16[16,336,128]{2,1,0:T(8,128)(2,1)} %copy-done.2), calls=%async_computation | async-start | bytes 2752512 | tf_op jit(solution)/shard_map/all_to_all | solution.py:447
  21.2 2.9 %copy-start.4 = (bf16[1,1281,2560]{2,1,0:T(8,128)(2,1)S(1)}, bf16[1,1281,2560]{2,1,0:T(8,128)(2,1)}, u32[]{:S(2)}) copy-start(bf16[1,1281,2560]{2,1,0:T(8,128)(2,1)} %param.19) | copy-start | bytes 19676164
  43.8 2.8 %copy-start.6 = (bf16[2560,1280]{1,0:T(8,128)(2,1)}, bf16[2560,1280]{1,0:T(8,128)(2,1)S(1)}, u32[]{:S(2)}) copy-start(bf16[2560,1280]{1,0:T(8,128)(2,1)S(1)} %get-tuple-element.25.refs_0_) | copy-start | bytes 19660804
  46.6 2.0 copy-start.7
  63.1 1.1 copy-start.1
  64.2 11.9 %copy-start.5 = (s32[8]{0:T(128)S(1)}, s32[8]{0:T(128)}, u32[]{:S(2)}) copy-start(s32[8]{0:T(128)} %bands_ref.1) | copy-start | bytes 100
  64.2 32.0 %all-to-all-start.1 = ((bf16[16,336,128]{2,1,0:T(8,128)(2,1)}), bf16[16,336,128]{2,1,0:T(8,128)(2,1)}, u32[]{:S(2)}, u32[]{:S(2)}) async-start(bf16[16,336,128]{2,1,0:T(8,128)(2,1)} %copy-done.1), calls=%async_computation.1 | async-start | bytes 2752512 | tf_op jit(solution)/shard_map/all_to_all | solution.py:447
where the time goes:
time: 261 us; the launch traced here: 260 us
  blocking collectives  150 us (57%)
  Pallas kernels  40.5 us (16%)
  waiting for transfers between devices  28.4 us (11%)
  starting transfers between devices  23.9 us (9%)
  local copies, waits for them, and re-layouts  16.5 us (6%)
    all_to_all x1, blocking collectives, per_device(): lax.all_to_all(outgoing, axes, split_axis=0, concat_axis=0, tiled=True)  150 us
    all_to_all x2, waiting for transfers between devices, exchange(): lax.all_to_all(rows, axes, split_axis=0, concat_axis=0, tiled=True, axis_...  28.4 us
    pallas_call x1, Pallas kernels, make_tables(): pl.pallas_call(functools.partial(table_kernel, plan), grid=(latitudes //...  19.7 us
    all_to_all x2, starting transfers between devices, exchange(): lax.all_to_all(rows, axes, split_axis=0, concat_axis=0, tiled=True, axis_...  16.2 us
    unnamed x33, local copies, waits for them, and re-layouts  14.4 us
    pallas_call x1, Pallas kernels, to_bands(): pl.pallas_call(functools.partial(grid_kernel, plan, levels, latitudes, de...  11.7 us
    pallas_call x1, Pallas kernels, filter_rows(): pl.pallas_call(functools.partial(filter_kernel, plan, levels), out_shape=...  5.87 us
    ppermute x2, starting transfers between devices, per_device(): far_blocks = [lax.ppermute(part, axes, far) for part in own]  5.33 us
  transfers between devices with their start and end apart: 6, of which 2 were waited for; matrix products, arithmetic and copies ran while one was open for 0% of the time, Pallas kernels for 9%

commit v1 on v0

--- a/solution.py
+++ b/solution.py
@@ -78,6 +78,48 @@
                 result = jnp.where(here, base + message * count + fold - start, result)
             base += self.group * count
         return result
+
+
+def cast_kernel(info_ref, blocks_ref, *refs):
+    *outs, held_ref, cast_ref, in_sems, out_sems = refs
+    total, each = blocks_ref.shape[0], outs[0].shape[0]
+    part = each // 2 if each % 2 == 0 else each
+    arrivals, departures = [], []
+    for fold in range(0, total, part):
+        piece, inside = fold // each, fold % each
+        start = jnp.where(info_ref[0] == 1, total - (piece + 1) * each, piece * each) + inside
+        at, here = len(arrivals), pl.ds(fold, part)
+        arrivals.append(pltpu.make_async_copy(blocks_ref.at[pl.ds(start, part)], held_ref.at[here], in_sems.at[at]))
+        arrivals[at].start()
+        there = outs[piece].at[pl.ds(inside, part)]
+        departures.append(pltpu.make_async_copy(cast_ref.at[here], there, out_sems.at[at]))
+    for at, fold in enumerate(range(0, total, part)):
+        arrivals[at].wait()
+        cast_ref[fold:fold + part] = held_ref[fold:fold + part].astype(BF)
+        departures[at].start()
+    for departure in departures:
+        departure.wait()
+
+
+def cast_blocks(blocks, info, pieces):
+    each = blocks.shape[0] // pieces
+    steps = pieces * (2 if each % 2 == 0 else 1)
+    anywhere = pl.BlockSpec(memory_space=pl.ANY)
+    return pl.pallas_call(
+        cast_kernel,
+        out_shape=[jax.ShapeDtypeStruct((each, *blocks.shape[1:]), BF)] * pieces,
+        in_specs=[pl.BlockSpec(memory_space=pltpu.SMEM), anywhere],
+        out_specs=[anywhere] * pieces,
+        scratch_shapes=[
+            pltpu.VMEM(blocks.shape, F32),
+            pltpu.VMEM(blocks.shape, BF),
+            pltpu.SemaphoreType.DMA((steps,)),
+            pltpu.SemaphoreType.DMA((steps,)),
+        ],
+        compiler_params=pltpu.CompilerParams(vmem_limit_bytes=56 * 1024 * 1024),
+        cost_estimate=pl.CostEstimate(flops=1, bytes_accessed=6 * blocks.size, transcendentals=0),
+        name="cast_blocks",
+    )(info, blocks)
 
 
 def pack_kernel(plan, levels, info_ref, slot_ref, control_ref, out_ref):
@@ -451,12 +493,7 @@
     far = [(d, (3 - d // plane) * plane + d % plane) for d in whole]
     near = [(d, d // plane * plane + plane - 1 - d % plane) for d in whole]
     pieces = 2 if block % 2 == 0 else 1
-    each = block // pieces
-    own = []
-    for fold in range(0, block, each):
-        start = jnp.where(is_high == 1, block - fold - each, fold)
-        own.append(lax.dynamic_slice_in_dim(covariance, start, each, 0).astype(BF))
-        own[-1], covariance = lax.optimization_barrier((own[-1], covariance))
+    own = cast_blocks(covariance, is_high[None], pieces)
     *own, control = lax.optimization_barrier((*own, control))
     far_blocks = [lax.ppermute(part, axes, far) for part in own]
     near_blocks = [lax.ppermute(part, axes, near) for part in own]

time: 261 us -> 256 us (0.981)
  local copies, waits for them, and re-layouts: 16.5 us -> 10.7 us
    unnamed x33 -> x19, local copies, waits for them, and re-layouts: 14.4 us -> 10.4 us
  transfers between devices with their start and end apart: 6 -> 6, of which waited for: 2 -> 2; matrix products, arithmetic and copies ran while one was open for 0% -> 1% of each run, Pallas kernels for 9% -> 9%
where the time goes in v1:
time: 256 us
  blocking collectives  149 us (58%)
  Pallas kernels  42.2 us (16%)
  waiting for transfers between devices  28.5 us (11%)
  starting transfers between devices  23.2 us (9%)
  local copies, waits for them, and re-layouts  10.7 us (4%)
    all_to_all x1, blocking collectives, per_device(): lax.all_to_all(outgoing, axes, split_axis=0, concat_axis=0, tiled=True)  149 us
    all_to_all x2, waiting for transfers between devices, exchange(): lax.all_to_all(rows, axes, split_axis=0, concat_axis=0, tiled=True, axis_...  28.5 us
    pallas_call x1, Pallas kernels, make_tables(): pl.pallas_call(functools.partial(table_kernel, plan), grid=(latitudes //...  19.7 us
    all_to_all x2, starting transfers between devices, exchange(): lax.all_to_all(rows, axes, split_axis=0, concat_axis=0, tiled=True, axis_...  15.4 us
    pallas_call x1, Pallas kernels, to_bands(): pl.pallas_call(functools.partial(grid_kernel, plan, levels, latitudes, de...  10.8 us
    unnamed x19, local copies, waits for them, and re-layouts  10.4 us
    ppermute x2, starting transfers between devices, per_device(): far_blocks = [lax.ppermute(part, axes, far) for part in own]  5.47 us
  transfers between devices with their start and end apart: 6, of which 2 were waited for; matrix products, arithmetic and copies ran while one was open for 1% of the time, Pallas kernels for 9%

profile of v1, /device:TPU:0, one launch (start us, length us, event | category | flops | bytes accessed | tf_op | source)
XLA Modules:
  0.0 256.0 jit_solution(4651752485019448246)
XLA Ops:
  0.0 2.6 %cast_blocks.1 = (bf16[20,128,128]{2,1,0:T(8,128)(2,1)}, bf16[20,128,128]{2,1,0:T(8,128)(2,1)}) custom-call(s32[1]{0:T(128)} %bitcast.5.info_ref, f32[40,128,128]{2,1,0:T(8,128)} %blocks_ref.1), custom_call_target="tpu_custom_call" | custom-call | flops 1 | bytes 3932160 | tf_op jit(solution)/shard_map/cast_blocks/pallas_call | solution.py:108
  2.6 0.0 copy-start.5
  2.7 5.1 %collective-permute-start.2 = (bf16[20,128,128]{2,1,0:T(8,128)(2,1)}, bf16[20,128,128]{2,1,0:T(8,128)(2,1)S(1)}, u32[]{:S(2)}, u32[]{:S(2)}) collective-permute-start(bf16[20,128,128]{2,1,0:T(8,128)(2,1)} %get-tuple-element.21), channel_id=1, source_target_pairs={{0,24},{1,25},{2,26},{3,27},{4,28},{5,29},{6,30},{7,31},{8,16},{9,... | collective-permute-start | bytes 1966088 | tf_op jit(solution)/shard_map/ppermute | solution.py:498
  7.8 1.6 collective-permute-start
  9.4 0.4 collective-permute-start.3
  9.7 0.7 collective-permute-start.1
  11.1 0.8 compare_select_fusion.1
  11.8 0.2 broadcast_in_dim.18.slot_ref
  12.1 4.0 %pack_rows.1 = bf16[16,336,128]{2,1,0:T(8,128)(2,1)} custom-call(s32[1]{0:T(128)} %copy.20.info_ref, s32[1280,1]{1,0:T(8,128)S(1)} %broadcast_in_dim.18.slot_ref, bf16[1281,512]{1,0:T(8,128)(2,1)S(1)} %bitcast.18), custom_call_target="tpu_custom_call" | custom-call | flops 1 | bytes 1 | tf_op jit(solution)/shard_map/pack_rows/pallas_call | solution.py:161
  16.1 3.8 %all-to-all-start = ((bf16[16,336,128]{2,1,0:T(8,128)(2,1)}), bf16[16,336,128]{2,1,0:T(8,128)(2,1)S(1)}, u32[]{:S(2)}, u32[]{:S(2)}) async-start(bf16[16,336,128]{2,1,0:T(8,128)(2,1)} %pack_rows.1), calls=%async_computation | async-start | bytes 2752512 | tf_op jit(solution)/shard_map/all_to_all | solution.py:489
  20.0 2.9 %copy-done.1 = bf16[1,1281,2560]{2,1,0:T(8,128)(2,1)S(1)} copy-done((bf16[1,1281,2560]{2,1,0:T(8,128)(2,1)S(1)}, bf16[1,1281,2560]{2,1,0:T(8,128)(2,1)}, u32[]{:S(2)}) %copy-start.1) | copy-done | bytes 6558744
  22.9 19.7 %make_tables.1 = (bf16[2560,1280]{1,0:T(8,128)(2,1)S(1)}, bf16[2560,768]{1,0:T(8,128)(2,1)S(1)}) custom-call(s32[1,1280]{1,0:T(1,128)S(1)} %broadcast_in_dim.16.upper_ref, s32[1,768]{1,0:T(1,128)S(1)} %broadcast_in_dim.17.lower_ref, bf16[1281,2560]{1,0:T(8,128)(2,1)S(1)} %bitcast.19), custom_call_target="tpu_custom_call" | custom-call | flops 134322585600 | bytes 6558720 | tf_op jit(solution)/shard_map/make_tables/pallas_call | solution.py:203
  42.6 2.8 %copy-done.3 = bf16[2560,1280]{1,0:T(8,128)(2,1)} copy-done((bf16[2560,1280]{1,0:T(8,128)(2,1)}, bf16[2560,1280]{1,0:T(8,128)(2,1)S(1)}, u32[]{:S(2)}) %copy-start.3) | copy-done | bytes 6553624
  45.4 2.0 copy-done.4
  47.4 0.1 pad_add_fusion.1.info_ref
  47.5 8.8 %all-to-all-done.rows_ref = bf16[16,336,128]{2,1,0:T(8,128)(2,1)S(1)} async-done(((bf16[16,336,128]{2,1,0:T(8,128)(2,1)}), bf16[16,336,128]{2,1,0:T(8,128)(2,1)S(1)}, u32[]{:S(2)}, u32[]{:S(2)}) %all-to-all-start) | async-done | bytes 1376288 | tf_op jit(solution)/shard_map/all_to_all | solution.py:489
  56.2 5.0 %filter_rows.1 = bf16[16,336,128]{2,1,0:T(8,128)(2,1)} custom-call(s32[2]{0:T(128)S(1)} %pad_add_fusion.1.info_ref, bf16[16,336,128]{2,1,0:T(8,128)(2,1)S(1)} %all-to-all-done.rows_ref, bf16[20,128,128]{2,1,0:T(8,128)(2,1)S(1)} %collective-permute-done.refs_0_, bf16[20,128,128]{2,1,0:T(8,128)(2,1)} %collective-permute-done.1.refs_1_, ...), custom_call_target="tpu_custom_call" | custom-call | flops 1342177280 | bytes 5373952 | tf_op jit(solution)/shard_map/filter_rows/pallas_call | solution.py:329
  61.3 11.6 %all-to-all-start.1 = ((bf16[16,336,128]{2,1,0:T(8,128)(2,1)}), bf16[16,336,128]{2,1,0:T(8,128)(2,1)S(1)}, u32[]{:S(2)}, u32[]{:S(2)}) async-start(bf16[16,336,128]{2,1,0:T(8,128)(2,1)} %filter_rows.1), calls=%async_computation.1 | async-start | bytes 2752512 | tf_op jit(solution)/shard_map/all_to_all | solution.py:489
  73.0 0.2 reduce-window.9
  73.2 0.1 pad_add_fusion.info_ref
  73.2 19.8 %all-to-all-done.1.part_ref = bf16[16,336,128]{2,1,0:T(8,128)(2,1)S(1)} async-done(((bf16[16,336,128]{2,1,0:T(8,128)(2,1)}), bf16[16,336,128]{2,1,0:T(8,128)(2,1)S(1)}, u32[]{:S(2)}, u32[]{:S(2)}) %all-to-all-start.1) | async-done | bytes 1376288 | tf_op jit(solution)/shard_map/all_to_all | solution.py:489
  93.0 10.8 %grid_bands.1 = bf16[32,2,400,128]{3,2,1,0:T(8,128)(2,1)} custom-call(s32[2]{0:T(128)S(1)} %pad_add_fusion.info_ref, s32[8]{0:T(128)S(1)} %bitcast_subtract_fusion.starts_ref, s32[8]{0:T(128)S(1)} %copy-done.2, bf16[16,336,128]{2,1,0:T(8,128)(2,1)S(1)} %all-to-all-done.1.part_ref, bf16[2560,1280]{1,0:T(8,128)(2,1)} %copy-done.3, bf16[2560,768]{1,0:T(8,128)(2,1)} %copy-done.4), custom_call_target="tpu_custom_call" | custom-call | flops 5368709120 | bytes 17039360 | tf_op jit(solution)/shard_map/grid_bands/pallas_call | solution.py:447
  103.8 149.4 %all_to_all.15 = bf16[64,400,128]{2,1,0:T(8,128)(2,1)S(1)} all-to-all(bf16[64,400,128]{2,1,0:T(8,128)(2,1)} %bitcast.21), channel_id=1, replica_groups=mesh['wave'=8,'lev'=4] {'wave','lev'}, dimensions={0} | all-to-all | bytes 13107200 | tf_op jit(solution)/shard_map/all_to_all | solution.py:529
  253.2 2.8 %copy.21 = bf16[64,400,128]{2,1,0:T(8,128)(2,1)} copy(bf16[64,400,128]{2,1,0:T(8,128)(2,1)S(1)} %all_to_all.15) | data formatting | bytes 13107200
  (23 shorter events, 0.1 us)
Async XLA Ops:
  0.0 12.1 %copy-start = (bf16[1,1281,512]{2,1,0:T(8,128)(2,1)S(1)}, bf16[1,1281,512]{2,1,0:T(8,128)(2,1)}, u32[]{:S(2)}) copy-start(bf16[1,1281,512]{2,1,0:T(8,128)(2,1)} %param.17) | copy-start | bytes 3935236
  2.6 17.3 %copy-start.5 = (s32[1280]{0:T(1024)S(1)}, s32[1280]{0:T(1024)}, u32[]{:S(2)}) copy-start(s32[1280]{0:T(1024)} %constant.141.clone) | copy-start | bytes 15364
  2.6 17.3 %copy-start.6 = (s32[1280]{0:T(1024)S(1)}, s32[1280]{0:T(1024)}, u32[]{:S(2)}) copy-start(s32[1280]{0:T(1024)} %constant.140.clone) | copy-start | bytes 15364
  2.6 17.3 %copy-start.7 = (s32[1280]{0:T(1024)S(1)}, s32[1280]{0:T(1024)}, u32[]{:S(2)}) copy-start(s32[1280]{0:T(1024)} %constant.139.clone) | copy-start | bytes 15364
  2.7 17.3 %copy-start.8 = (pred[1280]{0:T(1024)(128)(4,1)S(1)}, pred[1280]{0:T(1024)(128)(4,1)}, u32[]{:S(2)}) copy-start(pred[1280]{0:T(1024)(128)(4,1)} %constant.142.clone) | copy-start | bytes 3844
  2.7 53.6 %collective-permute-start.2 = (bf16[20,128,128]{2,1,0:T(8,128)(2,1)}, bf16[20,128,128]{2,1,0:T(8,128)(2,1)S(1)}, u32[]{:S(2)}, u32[]{:S(2)}) collective-permute-start(bf16[20,128,128]{2,1,0:T(8,128)(2,1)} %get-tuple-element.21), channel_id=1, source_target_pairs={{0,24},{1,25},{2,26},{3,27},{4,28},{5,29},{6,30},{7,31},{8,16},{9,... | collective-permute-start | bytes 1966088 | tf_op jit(solution)/shard_map/ppermute | solution.py:498
  7.8 48.4 %collective-permute-start = (bf16[20,128,128]{2,1,0:T(8,128)(2,1)}, bf16[20,128,128]{2,1,0:T(8,128)(2,1)S(1)}, u32[]{:S(2)}, u32[]{:S(2)}) collective-permute-start(bf16[20,128,128]{2,1,0:T(8,128)(2,1)} %get-tuple-element.21), channel_id=1, source_target_pairs={{0,7},{1,6},{2,5},{3,4},{4,3},{5,2},{6,1},{7,0},{8,15},{9,14},{10,... | collective-permute-start | bytes 1966088 | tf_op jit(solution)/shard_map/ppermute | solution.py:499
  9.4 46.8 %collective-permute-start.3 = (bf16[20,128,128]{2,1,0:T(8,128)(2,1)}, bf16[20,128,128]{2,1,0:T(8,128)(2,1)S(1)}, u32[]{:S(2)}, u32[]{:S(2)}) collective-permute-start(bf16[20,128,128]{2,1,0:T(8,128)(2,1)} %get-tuple-element.22), channel_id=1, source_target_pairs={{0,24},{1,25},{2,26},{3,27},{4,28},{5,29},{6,30},{7,31},{8,16},{9,... | collective-permute-start | bytes 1966088 | tf_op jit(solution)/shard_map/ppermute | solution.py:498
  9.7 46.5 %collective-permute-start.1 = (bf16[20,128,128]{2,1,0:T(8,128)(2,1)}, bf16[20,128,128]{2,1,0:T(8,128)(2,1)}, u32[]{:S(2)}, u32[]{:S(2)}) collective-permute-start(bf16[20,128,128]{2,1,0:T(8,128)(2,1)} %get-tuple-element.22), channel_id=1, source_target_pairs={{0,7},{1,6},{2,5},{3,4},{4,3},{5,2},{6,1},{7,0},{8,15},{9,14},{10,... | collective-permute-start | bytes 1966088 | tf_op jit(solution)/shard_map/ppermute | solution.py:499
  16.1 40.1 %all-to-all-start = ((bf16[16,336,128]{2,1,0:T(8,128)(2,1)}), bf16[16,336,128]{2,1,0:T(8,128)(2,1)S(1)}, u32[]{:S(2)}, u32[]{:S(2)}) async-start(bf16[16,336,128]{2,1,0:T(8,128)(2,1)} %pack_rows.1), calls=%async_computation | async-start | bytes 2752512 | tf_op jit(solution)/shard_map/all_to_all | solution.py:489
  20.0 2.9 %copy-start.1 = (bf16[1,1281,2560]{2,1,0:T(8,128)(2,1)S(1)}, bf16[1,1281,2560]{2,1,0:T(8,128)(2,1)}, u32[]{:S(2)}) copy-start(bf16[1,1281,2560]{2,1,0:T(8,128)(2,1)} %param.19) | copy-start | bytes 19676164
  42.6 2.8 %copy-start.3 = (bf16[2560,1280]{1,0:T(8,128)(2,1)}, bf16[2560,1280]{1,0:T(8,128)(2,1)S(1)}, u32[]{:S(2)}) copy-start(bf16[2560,1280]{1,0:T(8,128)(2,1)S(1)} %get-tuple-element.23.refs_0_) | copy-start | bytes 19660804
  45.4 2.0 copy-start.4
  56.2 16.8 %copy-start.2 = (s32[8]{0:T(128)S(1)}, s32[8]{0:T(128)}, u32[]{:S(2)}) copy-start(s32[8]{0:T(128)} %bands_ref.1) | copy-start | bytes 100
  61.3 31.7 %all-to-all-start.1 = ((bf16[16,336,128]{2,1,0:T(8,128)(2,1)}), bf16[16,336,128]{2,1,0:T(8,128)(2,1)S(1)}, u32[]{:S(2)}, u32[]{:S(2)}) async-start(bf16[16,336,128]{2,1,0:T(8,128)(2,1)} %filter_rows.1), calls=%async_computation.1 | async-start | bytes 2752512 | tf_op jit(solution)/shard_map/all_to_all | solution.py:489

commit v2 on v0

--- a/solution.py
+++ b/solution.py
@@ -78,6 +78,48 @@
                 result = jnp.where(here, base + message * count + fold - start, result)
             base += self.group * count
         return result
+
+
+def cast_kernel(plan, chunk, steps, info_ref, blocks_ref, out_ref, held_ref, cast_ref, in_sems, out_sems):
+    _, fold, count = chunk
+    start = jnp.where(info_ref[0] == 1, plan.block - fold - count, fold)
+    each = count // steps
+    arrivals, departures = [], []
+    for at in range(steps):
+        here = pl.ds(at * each, each)
+        arrivals.append(
+            pltpu.make_async_copy(blocks_ref.at[pl.ds(start + at * each, each)], held_ref.at[here], in_sems.at[at])
+        )
+        arrivals[at].start()
+        departures.append(pltpu.make_async_copy(cast_ref.at[here], out_ref.at[here], out_sems.at[at]))
+    for at in range(steps):
+        arrivals[at].wait()
+        cast_ref[at * each:(at + 1) * each] = held_ref[at * each:(at + 1) * each].astype(BF)
+        departures[at].start()
+    for departure in departures:
+        departure.wait()
+
+
+def cast_blocks(plan, at, blocks, info):
+    count = plan.chunks[at][2]
+    steps = 4 if count % 32 == 0 else 1
+    shape = (count, *blocks.shape[1:])
+    anywhere = pl.BlockSpec(memory_space=pl.ANY)
+    return pl.pallas_call(
+        functools.partial(cast_kernel, plan, plan.chunks[at], steps),
+        out_shape=jax.ShapeDtypeStruct(shape, BF),
+        in_specs=[pl.BlockSpec(memory_space=pltpu.SMEM), anywhere],
+        out_specs=anywhere,
+        scratch_shapes=[
+            pltpu.VMEM(shape, F32),
+            pltpu.VMEM(shape, BF),
+            pltpu.SemaphoreType.DMA((steps,)),
+            pltpu.SemaphoreType.DMA((steps,)),
+        ],
+        compiler_params=pltpu.CompilerParams(vmem_limit_bytes=56 * 1024 * 1024),
+        cost_estimate=pl.CostEstimate(flops=1, bytes_accessed=6 * count, transcendentals=0),
+        name="cast_blocks",
+    )(info, blocks)
 
 
 def pack_kernel(plan, levels, info_ref, slot_ref, control_ref, out_ref):
@@ -180,131 +222,122 @@
     return jnp.where((i // SUB == j % SUB) & (i % SUB == j // SUB), 1.0, 0.0).astype(BF)
 
 
-def filter_kernel(plan, levels, info_ref, rows_ref, *refs):
-    *blocks, out_ref, held_ref, x_ref, y_ref, z_ref, in_sems, out_sems = refs
-    pieces = len(blocks) // 2
-    each = plan.block // pieces
-    first_fold = info_ref[1].astype(F32)
+def filter_kernel(plan, at, levels, info_ref, rows_ref, near_ref, far_ref, *refs):
+    first, last = at == 0, at == len(plan.chunks) - 1
+    before_ref = None if first else refs[0]
+    out_ref, *after, held_ref, x_ref, y_ref, z_ref, in_sems, out_sems = refs[0 if first else 2:]
+    row0, fold0, count = plan.chunks[at]
+    height = ceil_to(2 * count, SUB)
+    groups = plan.group // SUB
+    first_fold = (info_ref[1] + fold0).astype(F32)
     swap = swap_matrix()
 
-    arrivals = []
-    for at, block in enumerate(blocks):
-        place = info_ref[0] if at < pieces else 1 - info_ref[0]
-        folds = pl.ds(at % pieces * each, each)
-        arrivals.append(pltpu.make_async_copy(block, held_ref.at[place, folds], in_sems.at[at]))
-        arrivals[at].start()
-
-    def low_matrix(fold):
-        return held_ref[0, fold]
-
-    def high_matrix(fold):
-        return held_ref[1, fold // each * each + each - 1 - fold % each]
-
-    def times(rows, matrix):
-        return lax.dot_general(rows, matrix, (((1,), (1,)), ((), ())), preferred_element_type=F32)
+    near = pltpu.make_async_copy(near_ref, held_ref.at[info_ref[0]], in_sems.at[0])
+    far = pltpu.make_async_copy(far_ref, held_ref.at[1 - info_ref[0]], in_sems.at[1])
+    near.start()
+    far.start()
 
     def turn(rows):
         return jnp.dot(swap, rows, preferred_element_type=F32)
 
-    groups = plan.group // SUB
-    held = plan.rows * SUB
-    for g in range(groups):
-        sources = slice(g * SUB, (g + 1) * SUB)
-        for r in range(0, plan.rows, SUB):
-            parts = []
-            for c in range(4):
-                start = c * plan.rows + r
-                parts.append(rows_ref[sources, start:start + SUB, :].reshape(SUB * SUB, levels))
-            x_ref[g * held + r * SUB:g * held + (r + SUB) * SUB, :] = turn(jnp.concatenate(parts, axis=1)).astype(BF)
-
-    for arrival in arrivals:
-        arrival.wait()
-
-    departures = []
-
-    def send(rows):
-        at = len(departures)
-        departures.append(pltpu.make_async_copy(z_ref.at[:, rows, :], out_ref.at[:, rows, :], out_sems.at[at]))
-        departures[at].start()
-
+    held = height * SUB
     tails = []
     for g in range(groups):
         sources = slice(g * SUB, (g + 1) * SUB)
+        for r in range(0, height, SUB):
+            parts = []
+            for c in range(4):
+                start = c * plan.rows + row0 + r
+                parts.append(rows_ref[sources, start:start + SUB, :].reshape(SUB * SUB, levels))
+            x_ref[g * held + r * SUB:g * held + (r + SUB) * SUB, :] = turn(jnp.concatenate(parts, axis=1)).astype(BF)
         tail = turn(rows_ref[sources, 4 * plan.rows:4 * plan.rows + SUB, :].reshape(SUB * SUB, levels))
         low = tail[4 * SUB:5 * SUB] * DIGIT + tail[5 * SUB:6 * SUB]
-        tails.append([tail[:4 * SUB].astype(BF), jnp.concatenate([low] * 4, axis=0), jnp.zeros((4 * SUB, levels), F32)])
-
-    for row0, fold0, count in plan.chunks:
-        height = ceil_to(2 * count, SUB)
-        for g in range(groups):
-            sources = slice(g * SUB, (g + 1) * SUB)
-            extra, low, kept = tails[g]
-            for i in range(count):
-                def stack(row):
-                    at = g * held + row * SUB
-                    return jnp.concatenate(
-                        [x_ref[at:at + SUB, c * levels:(c + 1) * levels] for c in range(4)], axis=0
-                    )
-
-                folded, high = stack(row0 + i), stack(row0 + count + i)
-                from_low = times(folded, low_matrix(fold0 + i))
-                from_high = times(jnp.concatenate([folded, high, extra], axis=0), high_matrix(fold0 + i))
-                fold = first_fold + (fold0 + i)
-                mixed = jnp.where(low <= fold, from_low, from_high[:4 * SUB])
-                kept = jnp.where(low == fold, from_high[8 * SUB:], kept)
-                for row, value in ((row0 + i, mixed), (row0 + count + i, from_high[4 * SUB:8 * SUB])):
-                    value = value.astype(BF)
-                    for c in range(4):
-                        y_ref[row * SUB:(row + 1) * SUB, c * levels:(c + 1) * levels] = value[c * SUB:(c + 1) * SUB]
-            tails[g][2] = kept
-            if height > 2 * count:
-                y_ref[(row0 + 2 * count) * SUB:(row0 + height) * SUB, :] = jnp.zeros(
-                    ((height - 2 * count) * SUB, 4 * levels), BF
-                )
-            for r in range(row0, row0 + height, SUB):
-                back = turn(y_ref[r * SUB:(r + SUB) * SUB, :]).astype(BF)
-                for c in range(4):
-                    start = c * plan.rows + r
-                    z_ref[sources, start:start + SUB, :] = back[:, c * levels:(c + 1) * levels].reshape(
-                        SUB, SUB, levels
-                    )
-        for c in range(4):
-            send(pl.ds(c * plan.rows + row0, height))
+        if first:
+            kept = jnp.zeros((4 * SUB, levels), F32)
+        else:
+            kept = before_ref[4 * SUB * g:4 * SUB * (g + 1), :]
+        tails.append((tail[:4 * SUB].astype(BF), jnp.concatenate([low] * 4, axis=0), kept))
+    near.wait()
+    far.wait()
+
     for g in range(groups):
         sources = slice(g * SUB, (g + 1) * SUB)
-        filled = jnp.concatenate([tails[g][2], jnp.zeros((12 * SUB, levels), F32)], axis=0).astype(BF)
-        z_ref[sources, 4 * plan.rows:4 * plan.rows + SUB, :] = turn(filled).astype(BF).reshape(SUB, SUB, levels)
-    send(pl.ds(4 * plan.rows, SUB))
+        extra, low, kept = tails[g]
+        for i in range(count):
+            def stack(row):
+                start = g * held + row * SUB
+                return [x_ref[start:start + SUB, c * levels:(c + 1) * levels] for c in range(4)]
+
+            rows = jnp.concatenate([*stack(i), *stack(count + i), extra], axis=0)
+            matrices = jnp.concatenate([held_ref[0, i], held_ref[1, count - 1 - i]], axis=0)
+            both = lax.dot_general(rows, matrices, (((1,), (1,)), ((), ())), preferred_element_type=F32)
+            from_low, from_high = both[:4 * SUB, :levels], both[:, levels:]
+            fold = first_fold + i
+            mixed = jnp.where(low <= fold, from_low, from_high[:4 * SUB])
+            kept = jnp.where(low == fold, from_high[8 * SUB:], kept)
+            for row, value in ((i, mixed), (count + i, from_high[4 * SUB:8 * SUB])):
+                value = value.astype(BF)
+                for c in range(4):
+                    y_ref[row * SUB:(row + 1) * SUB, c * levels:(c + 1) * levels] = value[c * SUB:(c + 1) * SUB]
+        if height > 2 * count:
+            y_ref[2 * count * SUB:height * SUB, :] = jnp.zeros(((height - 2 * count) * SUB, 4 * levels), BF)
+        for r in range(0, height, SUB):
+            back = turn(y_ref[r * SUB:(r + SUB) * SUB, :]).astype(BF)
+            for c in range(4):
+                z_ref[sources, c * height + r:c * height + r + SUB, :] = back[:, c * levels:(c + 1) * levels].reshape(
+                    SUB, SUB, levels
+                )
+        if last:
+            filled = jnp.concatenate([kept, jnp.zeros((12 * SUB, levels), F32)], axis=0).astype(BF)
+            z_ref[sources, 4 * height:4 * height + SUB, :] = turn(filled).astype(BF).reshape(SUB, SUB, levels)
+        else:
+            after[0][4 * SUB * g:4 * SUB * (g + 1), :] = kept
+
+    moves = [(c * height, c * plan.rows + row0, height) for c in range(4)]
+    if last:
+        moves.append((4 * height, 4 * plan.rows, SUB))
+    departures = [
+        pltpu.make_async_copy(z_ref.at[:, pl.ds(here, n), :], out_ref.at[:, pl.ds(there, n), :], out_sems.at[c])
+        for c, (here, there, n) in enumerate(moves)
+    ]
+    for departure in departures:
+        departure.start()
     for departure in departures:
         departure.wait()
 
 
-def filter_rows(plan, info, received, near_blocks, far_blocks):
+def filter_rows(plan, at, info, received, near, far, before):
     levels = received.shape[2]
-    blocks = [*near_blocks, *far_blocks]
+    count = plan.chunks[at][2]
+    height = ceil_to(2 * count, SUB)
+    last = at == len(plan.chunks) - 1
     smem, vmem = pl.BlockSpec(memory_space=pltpu.SMEM), pl.BlockSpec(memory_space=pltpu.VMEM)
     anywhere = pl.BlockSpec(memory_space=pl.ANY)
+    out_shape = [jax.ShapeDtypeStruct(received.shape, BF)]
+    if not last:
+        out_shape.append(jax.ShapeDtypeStruct((4 * plan.group, levels), F32))
     return pl.pallas_call(
-        functools.partial(filter_kernel, plan, levels),
-        out_shape=jax.ShapeDtypeStruct(received.shape, BF),
-        in_specs=[smem, vmem] + [anywhere] * len(blocks),
-        out_specs=anywhere,
+        functools.partial(filter_kernel, plan, at, levels),
+        out_shape=out_shape,
+        in_specs=[smem, vmem, anywhere, anywhere] + ([vmem, anywhere] if before else []),
+        out_specs=[anywhere] + [vmem] * (len(out_shape) - 1),
+        input_output_aliases={5: 0} if before else {},
         scratch_shapes=[
-            pltpu.VMEM((2, plan.block, levels, levels), BF),
-            pltpu.VMEM((plan.group * plan.rows, 4 * levels), BF),
-            pltpu.VMEM((plan.rows * SUB, 4 * levels), BF),
-            pltpu.VMEM(received.shape, BF),
-            pltpu.SemaphoreType.DMA((len(blocks),)),
-            pltpu.SemaphoreType.DMA((4 * len(plan.chunks) + 1,)),
+            pltpu.VMEM((2, count, levels, levels), BF),
+            pltpu.VMEM((plan.group * height, 4 * levels), BF),
+            pltpu.VMEM((height * SUB, 4 * levels), BF),
+            pltpu.VMEM((plan.group, 4 * height + SUB, levels), BF),
+            pltpu.SemaphoreType.DMA((2,)),
+            pltpu.SemaphoreType.DMA((5,)),
         ],
         compiler_params=pltpu.CompilerParams(vmem_limit_bytes=20 * 1024 * 1024),
         cost_estimate=pl.CostEstimate(
-            flops=2 * plan.group * 16 * plan.block * levels * levels * 4,
-            bytes_accessed=2 * 2 * received.size + 4 * plan.block * levels * levels,
+            flops=2 * plan.group * 16 * count * levels * levels * 4,
+            bytes_accessed=2 * 2 * received.size + 4 * count * levels * levels,
             transcendentals=0,
         ),
         name="filter_rows",
-    )(info, received, *blocks)
+    )(info, received, near, far, *before)
 
 
 def grid_kernel(plan, levels, latitudes, depth, level_cols, tile, info_ref, starts_ref, bands_ref, part_ref, *refs):
@@ -450,16 +483,15 @@
     whole = range(2 * group)
     far = [(d, (3 - d // plane) * plane + d % plane) for d in whole]
     near = [(d, d // plane * plane + plane - 1 - d % plane) for d in whole]
-    pieces = 2 if block % 2 == 0 else 1
-    each = block // pieces
-    own = []
-    for fold in range(0, block, each):
-        start = jnp.where(is_high == 1, block - fold - each, fold)
-        own.append(lax.dynamic_slice_in_dim(covariance, start, each, 0).astype(BF))
-        own[-1], covariance = lax.optimization_barrier((own[-1], covariance))
-    *own, control = lax.optimization_barrier((*own, control))
-    far_blocks = [lax.ppermute(part, axes, far) for part in own]
-    near_blocks = [lax.ppermute(part, axes, near) for part in own]
+    far_blocks, near_blocks = [], []
+
+    def swap_chunk(own):
+        far_blocks.append(lax.ppermute(own, axes, far))
+        near_blocks.append(lax.ppermute(own, axes, near))
+
+    own = cast_blocks(plan, 0, covariance, is_high[None])
+    own, control = lax.optimization_barrier((own, control))
+    swap_chunk(own)
 
     def fold_block(rank):
         rank = jnp.where(is_high == 1, group - 1 - rank, rank)
@@ -474,13 +506,22 @@
 
     upper, lower = slots_of(*plan.message_rows())
     sent = jnp.where(upper >= 0, upper, lower)
-    received = exchange(pack(plan, control[0], pair_order, sent[:, None]))
+    packed = pack(plan, control[0], pair_order, sent[:, None])
+    packed, legendre = lax.optimization_barrier((packed, legendre))
+    received = exchange(packed)
 
     tables = make_tables(plan, legendre[0], slots_of(*plan.transform_rows()))
+    for at in range(1, len(plan.chunks)):
+        covariance, tables = lax.optimization_barrier((covariance, tables))
+        swap_chunk(cast_blocks(plan, at, covariance, is_high[None]))
 
     info = jnp.stack([is_high, fold_block(me - group * is_high) * block])
     received, tables = lax.optimization_barrier((received, tables))
-    filtered = exchange(filter_rows(plan, info, received, near_blocks, far_blocks))
+    before = ()
+    for at, (near_block, far_block) in enumerate(zip(near_blocks, far_blocks)):
+        result, *extras = filter_rows(plan, at, info, received, near_block, far_block, before)
+        before = (*extras, result)
+    filtered = exchange(result)
 
     extra_block = lowest // block
     extra_message = fold_block(extra_block)

time: 261 us -> 254 us (0.973)
  local copies, waits for them, and re-layouts: 16.5 us -> 10.7 us
  Pallas kernels: 40.5 us -> 45.2 us
  waiting for transfers between devices: 28.4 us -> 24.1 us
    all_to_all x2, waiting for transfers between devices: 28.4 us -> 20.3 us  [exchange(): lax.all_to_all(rows, axes, split_axis=0, concat_axis=0, tiled=True, axis_...]
    pallas_call x1 -> x4, Pallas kernels: 5.87 us -> 10.7 us  [the longest x2 6.53 us: filter_rows(): pl.pallas_call(functools.partial(filter_kernel, plan, at, levels), out_sh...]
    unnamed x33 -> x27, local copies, waits for them, and re-layouts: 14.4 us -> 10.5 us
    ppermute x4, waiting for transfers between devices: 0.01 us -> 3.79 us  [the longest x2 3.78 us: swap_chunk(): far_blocks.append(lax.ppermute(own, axes, far))]
    all_to_all x2, starting transfers between devices: 16.2 us -> 13 us  [exchange(): lax.all_to_all(rows, axes, split_axis=0, concat_axis=0, tiled=True, axis_...]
  transfers between devices with their start and end apart: 6 -> 6, of which waited for: 2 -> 3; matrix products, arithmetic and copies ran while one was open for 0% -> 0% of each run, Pallas kernels for 9% -> 12%
where the time goes in v2:
time: 254 us; the launch traced here: 253 us
  blocking collectives  149 us (59%)
  Pallas kernels  45.2 us (18%)
  waiting for transfers between devices  24.1 us (9%)
  starting transfers between devices  22.4 us (9%)
  local copies, waits for them, and re-layouts  10.7 us (4%)
    all_to_all x1, blocking collectives, per_device(): lax.all_to_all(outgoing, axes, split_axis=0, concat_axis=0, tiled=True)  149 us
    all_to_all x2, waiting for transfers between devices, exchange(): lax.all_to_all(rows, axes, split_axis=0, concat_axis=0, tiled=True, axis_...  20.3 us
    pallas_call x1, Pallas kernels, make_tables(): pl.pallas_call(functools.partial(table_kernel, plan), grid=(latitudes //...  19.7 us
    all_to_all x2, starting transfers between devices, exchange(): lax.all_to_all(rows, axes, split_axis=0, concat_axis=0, tiled=True, axis_...  13 us
    pallas_call x1, Pallas kernels, to_bands(): pl.pallas_call(functools.partial(grid_kernel, plan, levels, latitudes, de...  10.8 us
    unnamed x27, local copies, waits for them, and re-layouts  10.5 us
    pallas_call x2, Pallas kernels, filter_rows(): pl.pallas_call(functools.partial(filter_kernel, plan, at, levels), out_sh...  6.53 us
    ppermute x2, starting transfers between devices, swap_chunk(): far_blocks.append(lax.ppermute(own, axes, far))  5.92 us
  transfers between devices with their start and end apart: 6, of which 3 were waited for; matrix products, arithmetic and copies ran while one was open for 0% of the time, Pallas kernels for 12%

profile of v2, /device:TPU:0, one launch (start us, length us, event | category | flops | bytes accessed | tf_op | source)
XLA Modules:
  0.0 253.1 jit_solution(3902661103627847272)
XLA Ops:
  0.1 2.4 cast_blocks.2
  2.5 5.1 %collective-permute-start.3 = (bf16[32,128,128]{2,1,0:T(8,128)(2,1)}, bf16[32,128,128]{2,1,0:T(8,128)(2,1)S(1)}, u32[]{:S(2)}, u32[]{:S(2)}) collective-permute-start(bf16[32,128,128]{2,1,0:T(8,128)(2,1)} %cast_blocks.2), channel_id=1, source_target_pairs={{0,24},{1,25},{2,26},{3,27},{4,28},{5,29},{6,30},{7,31},{8,16},{9,... | collective-permute-start | bytes 3145736 | tf_op jit(solution)/shard_map/ppermute | solution.py:489
  7.6 1.6 collective-permute-start.2
  10.0 0.2 broadcast_in_dim.19.slot_ref
  10.2 4.0 %pack_rows.1 = bf16[16,336,128]{2,1,0:T(8,128)(2,1)} custom-call(s32[1]{0:T(128)} %copy.22.info_ref, s32[1280,1]{1,0:T(8,128)S(1)} %broadcast_in_dim.19.slot_ref, bf16[1281,512]{1,0:T(8,128)(2,1)S(1)} %bitcast.17), custom_call_target="tpu_custom_call" | custom-call | flops 1 | bytes 1 | tf_op jit(solution)/shard_map/pack_rows/pallas_call | solution.py:161
  14.2 3.7 %all-to-all-start = ((bf16[16,336,128]{2,1,0:T(8,128)(2,1)}), bf16[16,336,128]{2,1,0:T(8,128)(2,1)S(1)}, u32[]{:S(2)}, u32[]{:S(2)}) async-start(bf16[16,336,128]{2,1,0:T(8,128)(2,1)} %pack_rows.1), calls=%async_computation | async-start | bytes 2752512 | tf_op jit(solution)/shard_map/all_to_all | solution.py:480
  18.0 2.9 %copy-done.1 = bf16[1,1281,2560]{2,1,0:T(8,128)(2,1)S(1)} copy-done((bf16[1,1281,2560]{2,1,0:T(8,128)(2,1)S(1)}, bf16[1,1281,2560]{2,1,0:T(8,128)(2,1)}, u32[]{:S(2)}) %copy-start.1) | copy-done | bytes 6558744
  20.9 19.7 %make_tables.1 = (bf16[2560,1280]{1,0:T(8,128)(2,1)S(1)}, bf16[2560,768]{1,0:T(8,128)(2,1)S(1)}) custom-call(s32[1,1280]{1,0:T(1,128)S(1)} %broadcast_in_dim.17.upper_ref, s32[1,768]{1,0:T(1,128)S(1)} %broadcast_in_dim.18.lower_ref, bf16[1281,2560]{1,0:T(8,128)(2,1)S(1)} %bitcast.18), custom_call_target="tpu_custom_call" | custom-call | flops 134322585600 | bytes 6558720 | tf_op jit(solution)/shard_map/make_tables/pallas_call | solution.py:203
  40.6 2.8 %copy-done.3 = bf16[2560,1280]{1,0:T(8,128)(2,1)} copy-done((bf16[2560,1280]{1,0:T(8,128)(2,1)}, bf16[2560,1280]{1,0:T(8,128)(2,1)S(1)}, u32[]{:S(2)}) %copy-start.3) | copy-done | bytes 6553624
  43.4 2.0 copy-done.4
  45.4 1.8 cast_blocks.3
  47.1 0.8 collective-permute-start.1
  47.9 1.9 collective-permute-start
  49.8 0.1 pad_add_fusion.1.info_ref
  49.9 0.5 all-to-all-done.rows_ref
  50.4 4.2 %filter_rows.2 = (bf16[16,336,128]{2,1,0:T(8,128)(2,1)}, f32[64,128]{1,0:T(8,128)S(1)}) custom-call(s32[2]{0:T(128)S(1)} %pad_add_fusion.1.info_ref, bf16[16,336,128]{2,1,0:T(8,128)(2,1)S(1)} %all-to-all-done.rows_ref, bf16[32,128,128]{2,1,0:T(8,128)(2,1)} %collective-permute-done.2.near_ref, bf16[32,128,128]{2,1,0:T(8,128)(2,1)S(1)} %collective-permute-done.3.far_ref), custom_call_target="tpu_custom_call" | custom-call | flops 1073741824 | bytes 4849664 | tf_op jit(solution)/shard_map/filter_rows/pallas_call | solution.py:319
  54.6 3.8 %collective-permute-done.1.far_ref = bf16[8,128,128]{2,1,0:T(8,128)(2,1)S(1)} collective-permute-done((bf16[8,128,128]{2,1,0:T(8,128)(2,1)}, bf16[8,128,128]{2,1,0:T(8,128)(2,1)S(1)}, u32[]{:S(2)}, u32[]{:S(2)}) %collective-permute-start.1) | collective-permute-done | bytes 262176 | tf_op jit(solution)/shard_map/ppermute | solution.py:489
  58.4 2.3 filter_rows.3
  60.8 9.3 %all-to-all-start.1 = ((bf16[16,336,128]{2,1,0:T(8,128)(2,1)}), bf16[16,336,128]{2,1,0:T(8,128)(2,1)S(1)}, u32[]{:S(2)}, u32[]{:S(2)}) async-start(bf16[16,336,128]{2,1,0:T(8,128)(2,1)} %filter_rows.3), calls=%async_computation.1 | async-start | bytes 2752512 | tf_op jit(solution)/shard_map/all_to_all | solution.py:480
  70.2 0.2 reduce-window.9
  70.4 19.8 %all-to-all-done.1.part_ref = bf16[16,336,128]{2,1,0:T(8,128)(2,1)S(1)} async-done(((bf16[16,336,128]{2,1,0:T(8,128)(2,1)}), bf16[16,336,128]{2,1,0:T(8,128)(2,1)S(1)}, u32[]{:S(2)}, u32[]{:S(2)}) %all-to-all-start.1) | async-done | bytes 1376288 | tf_op jit(solution)/shard_map/all_to_all | solution.py:480
  90.2 10.8 %grid_bands.1 = bf16[32,2,400,128]{3,2,1,0:T(8,128)(2,1)} custom-call(s32[2]{0:T(128)S(1)} %pad_add_fusion.info_ref, s32[8]{0:T(128)S(1)} %bitcast_subtract_fusion.starts_ref, s32[8]{0:T(128)S(1)} %copy-done.2, bf16[16,336,128]{2,1,0:T(8,128)(2,1)S(1)} %all-to-all-done.1.part_ref, bf16[2560,1280]{1,0:T(8,128)(2,1)} %copy-done.3, bf16[2560,768]{1,0:T(8,128)(2,1)} %copy-done.4), custom_call_target="tpu_custom_call" | custom-call | flops 5368709120 | bytes 17039360 | tf_op jit(solution)/shard_map/grid_bands/pallas_call | solution.py:438
  101.0 149.4 %all_to_all.15 = bf16[64,400,128]{2,1,0:T(8,128)(2,1)S(1)} all-to-all(bf16[64,400,128]{2,1,0:T(8,128)(2,1)} %bitcast.20), channel_id=1, replica_groups=mesh['wave'=8,'lev'=4] {'wave','lev'}, dimensions={0} | all-to-all | bytes 13107200 | tf_op jit(solution)/shard_map/all_to_all | solution.py:533
  250.4 2.8 %copy.23 = bf16[64,400,128]{2,1,0:T(8,128)(2,1)} copy(bf16[64,400,128]{2,1,0:T(8,128)(2,1)S(1)} %all_to_all.15) | data formatting | bytes 13107200
  (32 shorter events, 0.2 us)
Async XLA Ops:
  0.0 9.9 %copy-start.11 = (pred[1280]{0:T(1024)(128)(4,1)S(1)}, pred[1280]{0:T(1024)(128)(4,1)}, u32[]{:S(2)}) copy-start(pred[1280]{0:T(1024)(128)(4,1)} %constant.142.clone) | copy-start | bytes 3844
  0.0 9.9 %copy-start.5 = (s32[1280]{0:T(1024)S(1)}, s32[1280]{0:T(1024)}, u32[]{:S(2)}) copy-start(s32[1280]{0:T(1024)} %constant.141.clone) | copy-start | bytes 15364
  0.0 9.9 %copy-start.6 = (s32[1280]{0:T(1024)S(1)}, s32[1280]{0:T(1024)}, u32[]{:S(2)}) copy-start(s32[1280]{0:T(1024)} %constant.140.clone) | copy-start | bytes 15364
  0.0 9.9 %copy-start.7 = (s32[1280]{0:T(1024)S(1)}, s32[1280]{0:T(1024)}, u32[]{:S(2)}) copy-start(s32[1280]{0:T(1024)} %constant.139.clone) | copy-start | bytes 15364
  0.0 9.9 %copy-start.12 = (pred[1280]{0:T(1024)(128)(4,1)S(1)}, pred[1280]{0:T(1024)(128)(4,1)}, u32[]{:S(2)}) copy-start(pred[1280]{0:T(1024)(128)(4,1)} %constant.137.clone) | copy-start | bytes 3844
  0.0 9.9 %copy-start.8 = (s32[1280]{0:T(1024)S(1)}, s32[1280]{0:T(1024)}, u32[]{:S(2)}) copy-start(s32[1280]{0:T(1024)} %constant.136.clone) | copy-start | bytes 15364
  0.0 9.9 %copy-start.9 = (s32[1280]{0:T(1024)S(1)}, s32[1280]{0:T(1024)}, u32[]{:S(2)}) copy-start(s32[1280]{0:T(1024)} %constant.135.clone) | copy-start | bytes 15364
  0.0 9.9 %copy-start.10 = (s32[1280]{0:T(1024)S(1)}, s32[1280]{0:T(1024)}, u32[]{:S(2)}) copy-start(s32[1280]{0:T(1024)} %constant.134.clone) | copy-start | bytes 15364
  0.1 10.2 %copy-start = (bf16[1,1281,512]{2,1,0:T(8,128)(2,1)S(1)}, bf16[1,1281,512]{2,1,0:T(8,128)(2,1)}, u32[]{:S(2)}) copy-start(bf16[1,1281,512]{2,1,0:T(8,128)(2,1)} %param.17) | copy-start | bytes 3935236
  2.5 47.9 %collective-permute-start.3 = (bf16[32,128,128]{2,1,0:T(8,128)(2,1)}, bf16[32,128,128]{2,1,0:T(8,128)(2,1)S(1)}, u32[]{:S(2)}, u32[]{:S(2)}) collective-permute-start(bf16[32,128,128]{2,1,0:T(8,128)(2,1)} %cast_blocks.2), channel_id=1, source_target_pairs={{0,24},{1,25},{2,26},{3,27},{4,28},{5,29},{6,30},{7,31},{8,16},{9,... | collective-permute-start | bytes 3145736 | tf_op jit(solution)/shard_map/ppermute | solution.py:489
  7.6 42.8 %collective-permute-start.2 = (bf16[32,128,128]{2,1,0:T(8,128)(2,1)}, bf16[32,128,128]{2,1,0:T(8,128)(2,1)}, u32[]{:S(2)}, u32[]{:S(2)}) collective-permute-start(bf16[32,128,128]{2,1,0:T(8,128)(2,1)} %cast_blocks.2), channel_id=1, source_target_pairs={{0,7},{1,6},{2,5},{3,4},{4,3},{5,2},{6,1},{7,0},{8,15},{9,14},{10,... | collective-permute-start | bytes 3145736 | tf_op jit(solution)/shard_map/ppermute | solution.py:490
  14.2 36.2 %all-to-all-start = ((bf16[16,336,128]{2,1,0:T(8,128)(2,1)}), bf16[16,336,128]{2,1,0:T(8,128)(2,1)S(1)}, u32[]{:S(2)}, u32[]{:S(2)}) async-start(bf16[16,336,128]{2,1,0:T(8,128)(2,1)} %pack_rows.1), calls=%async_computation | async-start | bytes 2752512 | tf_op jit(solution)/shard_map/all_to_all | solution.py:480
  18.0 2.9 %copy-start.1 = (bf16[1,1281,2560]{2,1,0:T(8,128)(2,1)S(1)}, bf16[1,1281,2560]{2,1,0:T(8,128)(2,1)}, u32[]{:S(2)}) copy-start(bf16[1,1281,2560]{2,1,0:T(8,128)(2,1)} %param.19) | copy-start | bytes 19676164
  40.6 2.8 %copy-start.3 = (bf16[2560,1280]{1,0:T(8,128)(2,1)}, bf16[2560,1280]{1,0:T(8,128)(2,1)S(1)}, u32[]{:S(2)}) copy-start(bf16[2560,1280]{1,0:T(8,128)(2,1)S(1)} %get-tuple-element.31.refs_0_) | copy-start | bytes 19660804
  43.4 2.0 copy-start.4
  47.1 11.3 %collective-permute-start.1 = (bf16[8,128,128]{2,1,0:T(8,128)(2,1)}, bf16[8,128,128]{2,1,0:T(8,128)(2,1)S(1)}, u32[]{:S(2)}, u32[]{:S(2)}) collective-permute-start(bf16[8,128,128]{2,1,0:T(8,128)(2,1)} %cast_blocks.3), channel_id=1, source_target_pairs={{0,24},{1,25},{2,26},{3,27},{4,28},{5,29},{6,30},{7,31},{8,16},{9,... | collective-permute-start | bytes 786440 | tf_op jit(solution)/shard_map/ppermute | solution.py:489
  47.9 10.5 %collective-permute-start = (bf16[8,128,128]{2,1,0:T(8,128)(2,1)}, bf16[8,128,128]{2,1,0:T(8,128)(2,1)S(1)}, u32[]{:S(2)}, u32[]{:S(2)}) collective-permute-start(bf16[8,128,128]{2,1,0:T(8,128)(2,1)} %cast_blocks.3), channel_id=1, source_target_pairs={{0,7},{1,6},{2,5},{3,4},{4,3},{5,2},{6,1},{7,0},{8,15},{9,14},{10,... | collective-permute-start | bytes 786440 | tf_op jit(solution)/shard_map/ppermute | solution.py:490
  58.4 11.7 %copy-start.2 = (s32[8]{0:T(128)S(1)}, s32[8]{0:T(128)}, u32[]{:S(2)}) copy-start(s32[8]{0:T(128)} %bands_ref.1) | copy-start | bytes 100
  60.8 29.4 %all-to-all-start.1 = ((bf16[16,336,128]{2,1,0:T(8,128)(2,1)}), bf16[16,336,128]{2,1,0:T(8,128)(2,1)S(1)}, u32[]{:S(2)}, u32[]{:S(2)}) async-start(bf16[16,336,128]{2,1,0:T(8,128)(2,1)} %filter_rows.3), calls=%async_computation.1 | async-start | bytes 2752512 | tf_op jit(solution)/shard_map/all_to_all | solution.py:480

commit v3 on v2

--- a/solution.py
+++ b/solution.py
@@ -345,14 +345,14 @@
     upper_ref, lower_ref, *grids, cut_ref, sems, out_sems = refs[5:]
     waves = bands_ref.shape[0]
     groups = 4 * levels // level_cols
-    tiles = [slice(start, stop) for start, stop in zip(tile, tile[1:])]
+    tiles = [[slice(start, stop) for start, stop in zip(edges, edges[1:])] for edges in tile]
 
     def copy(half, at):
-        rows = tiles[at]
+        rows = tiles[half][at]
         return pltpu.make_async_copy(tables[half].at[rows], held_tables[half].at[rows], sems.at[half, at])
 
     for half in (1, 0):
-        for at in range(len(tiles)):
+        for at in range(len(tiles[half])):
             copy(half, at).start()
 
     base = 0
@@ -378,7 +378,7 @@
 
     def transform(half, at):
         copy(half, at).wait()
-        rows = tiles[at]
+        rows = tiles[half][at]
         grids[half][rows, :] = jnp.dot(
             held_tables[half][rows, :], (upper_ref, lower_ref)[half][...], preferred_element_type=F32
         )
@@ -411,13 +411,22 @@
                 done = []
         departure(half, w).start()
 
-    for at in range(len(tiles)):
+    for at in range(len(tiles[1])):
         transform(1, at)
-    for at in range(len(tiles)):
+    todo = [[w for w in range(waves)] for _ in range(2)]
+    made = 0
+    for at, rows in enumerate(tiles[0]):
         transform(0, at)
-        for w in range(at * waves // len(tiles), (at + 1) * waves // len(tiles)):
-            cut(1, w)
-    for w in range(waves):
+        for w in list(todo[1]):
+            if at > 0 or w < waves // 2:
+                cut(1, w)
+                todo[1].remove(w)
+        for w in list(todo[0]):
+            if depth * (w + 1) <= made:
+                cut(0, w)
+                todo[0].remove(w)
+        made = rows.stop
+    for w in todo[0]:
         cut(0, w)
     for half in range(2):
         for w in range(waves):
@@ -428,7 +437,8 @@
     latitudes = tables[0].shape[0]
     levels = part.shape[2]
     columns = 4 * levels
-    tile = [0] + list(range(latitudes // 5, latitudes + 1, 2 * latitudes // 5))
+    fifth = latitudes // 5
+    tile = [[0, 2 * fifth, 4 * fifth, latitudes], [0, fifth, 3 * fifth, latitudes]]
     smem, vmem = pl.BlockSpec(memory_space=pltpu.SMEM), pl.BlockSpec(memory_space=pltpu.VMEM)
     messages = bands.shape[0] * columns // level_cols
     grid = pltpu.VMEM((ceil_to(latitudes + depth, 8) + 8, columns), F32)
@@ -448,7 +458,7 @@
             grid,
             grid,
             pltpu.VMEM((messages, 2, depth, level_cols), BF),
-            pltpu.SemaphoreType.DMA((2, len(tile) - 1)),
+            pltpu.SemaphoreType.DMA((2, 3)),
             pltpu.SemaphoreType.DMA((2, bands.shape[0])),
         ],
         compiler_params=pltpu.CompilerParams(vmem_limit_bytes=limit),

time: 254 us -> 254 us (level)
  no operation moved by 1% of the time
where the time goes in v3:
time: 254 us; the launch traced here: 253 us
  blocking collectives  149 us (59%)
  Pallas kernels  45.2 us (18%)
  waiting for transfers between devices  24.1 us (9%)
  starting transfers between devices  22.4 us (9%)
  local copies, waits for them, and re-layouts  10.7 us (4%)
    all_to_all x1, blocking collectives, per_device(): lax.all_to_all(outgoing, axes, split_axis=0, concat_axis=0, tiled=True)  149 us
    all_to_all x2, waiting for transfers between devices, exchange(): lax.all_to_all(rows, axes, split_axis=0, concat_axis=0, tiled=True, axis_...  20.3 us
    pallas_call x1, Pallas kernels, make_tables(): pl.pallas_call(functools.partial(table_kernel, plan), grid=(latitudes //...  19.7 us
    all_to_all x2, starting transfers between devices, exchange(): lax.all_to_all(rows, axes, split_axis=0, concat_axis=0, tiled=True, axis_...  13 us
    pallas_call x1, Pallas kernels, to_bands(): pl.pallas_call(functools.partial(grid_kernel, plan, levels, latitudes, de...  10.8 us
    unnamed x27, local copies, waits for them, and re-layouts  10.5 us
    pallas_call x2, Pallas kernels, filter_rows(): pl.pallas_call(functools.partial(filter_kernel, plan, at, levels), out_sh...  6.54 us
    ppermute x2, starting transfers between devices, swap_chunk(): far_blocks.append(lax.ppermute(own, axes, far))  5.91 us
  transfers between devices with their start and end apart: 6, of which 3 were waited for; matrix products, arithmetic and copies ran while one was open for 0% of the time, Pallas kernels for 12%

profile of v3, /device:TPU:0, one launch (start us, length us, event | category | flops | bytes accessed | tf_op | source)
XLA Modules:
  0.0 253.1 jit_solution(5415878021041231777)
XLA Ops:
  0.1 2.4 cast_blocks.2
  2.5 5.1 %collective-permute-start.3 = (bf16[32,128,128]{2,1,0:T(8,128)(2,1)}, bf16[32,128,128]{2,1,0:T(8,128)(2,1)S(1)}, u32[]{:S(2)}, u32[]{:S(2)}) collective-permute-start(bf16[32,128,128]{2,1,0:T(8,128)(2,1)} %cast_blocks.2), channel_id=1, source_target_pairs={{0,24},{1,25},{2,26},{3,27},{4,28},{5,29},{6,30},{7,31},{8,16},{9,... | collective-permute-start | bytes 3145736 | tf_op jit(solution)/shard_map/ppermute | solution.py:499
  7.6 1.6 collective-permute-start.2
  10.0 0.2 broadcast_in_dim.19.slot_ref
  10.2 4.0 %pack_rows.1 = bf16[16,336,128]{2,1,0:T(8,128)(2,1)} custom-call(s32[1]{0:T(128)} %copy.22.info_ref, s32[1280,1]{1,0:T(8,128)S(1)} %broadcast_in_dim.19.slot_ref, bf16[1281,512]{1,0:T(8,128)(2,1)S(1)} %bitcast.17), custom_call_target="tpu_custom_call" | custom-call | flops 1 | bytes 1 | tf_op jit(solution)/shard_map/pack_rows/pallas_call | solution.py:161
  14.2 3.7 %all-to-all-start = ((bf16[16,336,128]{2,1,0:T(8,128)(2,1)}), bf16[16,336,128]{2,1,0:T(8,128)(2,1)S(1)}, u32[]{:S(2)}, u32[]{:S(2)}) async-start(bf16[16,336,128]{2,1,0:T(8,128)(2,1)} %pack_rows.1), calls=%async_computation | async-start | bytes 2752512 | tf_op jit(solution)/shard_map/all_to_all | solution.py:490
  18.0 2.9 %copy-done.1 = bf16[1,1281,2560]{2,1,0:T(8,128)(2,1)S(1)} copy-done((bf16[1,1281,2560]{2,1,0:T(8,128)(2,1)S(1)}, bf16[1,1281,2560]{2,1,0:T(8,128)(2,1)}, u32[]{:S(2)}) %copy-start.1) | copy-done | bytes 6558744
  20.9 19.7 %make_tables.1 = (bf16[2560,1280]{1,0:T(8,128)(2,1)S(1)}, bf16[2560,768]{1,0:T(8,128)(2,1)S(1)}) custom-call(s32[1,1280]{1,0:T(1,128)S(1)} %broadcast_in_dim.17.upper_ref, s32[1,768]{1,0:T(1,128)S(1)} %broadcast_in_dim.18.lower_ref, bf16[1281,2560]{1,0:T(8,128)(2,1)S(1)} %bitcast.18), custom_call_target="tpu_custom_call" | custom-call | flops 134322585600 | bytes 6558720 | tf_op jit(solution)/shard_map/make_tables/pallas_call | solution.py:203
  40.6 2.8 %copy-done.3 = bf16[2560,1280]{1,0:T(8,128)(2,1)} copy-done((bf16[2560,1280]{1,0:T(8,128)(2,1)}, bf16[2560,1280]{1,0:T(8,128)(2,1)S(1)}, u32[]{:S(2)}) %copy-start.3) | copy-done | bytes 6553624
  43.4 2.0 copy-done.4
  45.4 1.8 cast_blocks.3
  47.2 0.8 collective-permute-start.1
  47.9 1.9 collective-permute-start
  49.8 0.1 pad_add_fusion.1.info_ref
  49.9 0.5 all-to-all-done.rows_ref
  50.4 4.2 %filter_rows.2 = (bf16[16,336,128]{2,1,0:T(8,128)(2,1)}, f32[64,128]{1,0:T(8,128)S(1)}) custom-call(s32[2]{0:T(128)S(1)} %pad_add_fusion.1.info_ref, bf16[16,336,128]{2,1,0:T(8,128)(2,1)S(1)} %all-to-all-done.rows_ref, bf16[32,128,128]{2,1,0:T(8,128)(2,1)} %collective-permute-done.2.near_ref, bf16[32,128,128]{2,1,0:T(8,128)(2,1)S(1)} %collective-permute-done.3.far_ref), custom_call_target="tpu_custom_call" | custom-call | flops 1073741824 | bytes 4849664 | tf_op jit(solution)/shard_map/filter_rows/pallas_call | solution.py:319
  54.6 3.8 %collective-permute-done.1.far_ref = bf16[8,128,128]{2,1,0:T(8,128)(2,1)S(1)} collective-permute-done((bf16[8,128,128]{2,1,0:T(8,128)(2,1)}, bf16[8,128,128]{2,1,0:T(8,128)(2,1)S(1)}, u32[]{:S(2)}, u32[]{:S(2)}) %collective-permute-start.1) | collective-permute-done | bytes 262176 | tf_op jit(solution)/shard_map/ppermute | solution.py:499
  58.4 2.3 filter_rows.3
  60.8 9.3 %all-to-all-start.1 = ((bf16[16,336,128]{2,1,0:T(8,128)(2,1)}), bf16[16,336,128]{2,1,0:T(8,128)(2,1)S(1)}, u32[]{:S(2)}, u32[]{:S(2)}) async-start(bf16[16,336,128]{2,1,0:T(8,128)(2,1)} %filter_rows.3), calls=%async_computation.1 | async-start | bytes 2752512 | tf_op jit(solution)/shard_map/all_to_all | solution.py:490
  70.2 0.2 reduce-window.9
  70.4 19.8 %all-to-all-done.1.part_ref = bf16[16,336,128]{2,1,0:T(8,128)(2,1)S(1)} async-done(((bf16[16,336,128]{2,1,0:T(8,128)(2,1)}), bf16[16,336,128]{2,1,0:T(8,128)(2,1)S(1)}, u32[]{:S(2)}, u32[]{:S(2)}) %all-to-all-start.1) | async-done | bytes 1376288 | tf_op jit(solution)/shard_map/all_to_all | solution.py:490
  90.2 10.8 %grid_bands.1 = bf16[32,2,400,128]{3,2,1,0:T(8,128)(2,1)} custom-call(s32[2]{0:T(128)S(1)} %pad_add_fusion.info_ref, s32[8]{0:T(128)S(1)} %bitcast_subtract_fusion.starts_ref, s32[8]{0:T(128)S(1)} %copy-done.2, bf16[16,336,128]{2,1,0:T(8,128)(2,1)S(1)} %all-to-all-done.1.part_ref, bf16[2560,1280]{1,0:T(8,128)(2,1)} %copy-done.3, bf16[2560,768]{1,0:T(8,128)(2,1)} %copy-done.4), custom_call_target="tpu_custom_call" | custom-call | flops 5368709120 | bytes 17039360 | tf_op jit(solution)/shard_map/grid_bands/pallas_call | solution.py:448
  101.0 149.4 %all_to_all.15 = bf16[64,400,128]{2,1,0:T(8,128)(2,1)S(1)} all-to-all(bf16[64,400,128]{2,1,0:T(8,128)(2,1)} %bitcast.20), channel_id=1, replica_groups=mesh['wave'=8,'lev'=4] {'wave','lev'}, dimensions={0} | all-to-all | bytes 13107200 | tf_op jit(solution)/shard_map/all_to_all | solution.py:543
  250.3 2.8 %copy.23 = bf16[64,400,128]{2,1,0:T(8,128)(2,1)} copy(bf16[64,400,128]{2,1,0:T(8,128)(2,1)S(1)} %all_to_all.15) | data formatting | bytes 13107200
  (32 shorter events, 0.2 us)
Async XLA Ops:
  0.0 9.9 %copy-start.11 = (pred[1280]{0:T(1024)(128)(4,1)S(1)}, pred[1280]{0:T(1024)(128)(4,1)}, u32[]{:S(2)}) copy-start(pred[1280]{0:T(1024)(128)(4,1)} %constant.142.clone) | copy-start | bytes 3844
  0.0 9.9 %copy-start.5 = (s32[1280]{0:T(1024)S(1)}, s32[1280]{0:T(1024)}, u32[]{:S(2)}) copy-start(s32[1280]{0:T(1024)} %constant.141.clone) | copy-start | bytes 15364
  0.0 9.9 %copy-start.6 = (s32[1280]{0:T(1024)S(1)}, s32[1280]{0:T(1024)}, u32[]{:S(2)}) copy-start(s32[1280]{0:T(1024)} %constant.140.clone) | copy-start | bytes 15364
  0.0 9.9 %copy-start.7 = (s32[1280]{0:T(1024)S(1)}, s32[1280]{0:T(1024)}, u32[]{:S(2)}) copy-start(s32[1280]{0:T(1024)} %constant.139.clone) | copy-start | bytes 15364
  0.0 9.9 %copy-start.12 = (pred[1280]{0:T(1024)(128)(4,1)S(1)}, pred[1280]{0:T(1024)(128)(4,1)}, u32[]{:S(2)}) copy-start(pred[1280]{0:T(1024)(128)(4,1)} %constant.137.clone) | copy-start | bytes 3844
  0.0 9.9 %copy-start.8 = (s32[1280]{0:T(1024)S(1)}, s32[1280]{0:T(1024)}, u32[]{:S(2)}) copy-start(s32[1280]{0:T(1024)} %constant.136.clone) | copy-start | bytes 15364
  0.0 9.9 %copy-start.9 = (s32[1280]{0:T(1024)S(1)}, s32[1280]{0:T(1024)}, u32[]{:S(2)}) copy-start(s32[1280]{0:T(1024)} %constant.135.clone) | copy-start | bytes 15364
  0.0 9.9 %copy-start.10 = (s32[1280]{0:T(1024)S(1)}, s32[1280]{0:T(1024)}, u32[]{:S(2)}) copy-start(s32[1280]{0:T(1024)} %constant.134.clone) | copy-start | bytes 15364
  0.1 10.2 %copy-start = (bf16[1,1281,512]{2,1,0:T(8,128)(2,1)S(1)}, bf16[1,1281,512]{2,1,0:T(8,128)(2,1)}, u32[]{:S(2)}) copy-start(bf16[1,1281,512]{2,1,0:T(8,128)(2,1)} %param.17) | copy-start | bytes 3935236
  2.5 47.9 %collective-permute-start.3 = (bf16[32,128,128]{2,1,0:T(8,128)(2,1)}, bf16[32,128,128]{2,1,0:T(8,128)(2,1)S(1)}, u32[]{:S(2)}, u32[]{:S(2)}) collective-permute-start(bf16[32,128,128]{2,1,0:T(8,128)(2,1)} %cast_blocks.2), channel_id=1, source_target_pairs={{0,24},{1,25},{2,26},{3,27},{4,28},{5,29},{6,30},{7,31},{8,16},{9,... | collective-permute-start | bytes 3145736 | tf_op jit(solution)/shard_map/ppermute | solution.py:499
  7.6 42.8 %collective-permute-start.2 = (bf16[32,128,128]{2,1,0:T(8,128)(2,1)}, bf16[32,128,128]{2,1,0:T(8,128)(2,1)}, u32[]{:S(2)}, u32[]{:S(2)}) collective-permute-start(bf16[32,128,128]{2,1,0:T(8,128)(2,1)} %cast_blocks.2), channel_id=1, source_target_pairs={{0,7},{1,6},{2,5},{3,4},{4,3},{5,2},{6,1},{7,0},{8,15},{9,14},{10,... | collective-permute-start | bytes 3145736 | tf_op jit(solution)/shard_map/ppermute | solution.py:500
  14.2 36.2 %all-to-all-start = ((bf16[16,336,128]{2,1,0:T(8,128)(2,1)}), bf16[16,336,128]{2,1,0:T(8,128)(2,1)S(1)}, u32[]{:S(2)}, u32[]{:S(2)}) async-start(bf16[16,336,128]{2,1,0:T(8,128)(2,1)} %pack_rows.1), calls=%async_computation | async-start | bytes 2752512 | tf_op jit(solution)/shard_map/all_to_all | solution.py:490
  18.0 2.9 %copy-start.1 = (bf16[1,1281,2560]{2,1,0:T(8,128)(2,1)S(1)}, bf16[1,1281,2560]{2,1,0:T(8,128)(2,1)}, u32[]{:S(2)}) copy-start(bf16[1,1281,2560]{2,1,0:T(8,128)(2,1)} %param.19) | copy-start | bytes 19676164
  40.6 2.8 %copy-start.3 = (bf16[2560,1280]{1,0:T(8,128)(2,1)}, bf16[2560,1280]{1,0:T(8,128)(2,1)S(1)}, u32[]{:S(2)}) copy-start(bf16[2560,1280]{1,0:T(8,128)(2,1)S(1)} %get-tuple-element.31.refs_0_) | copy-start | bytes 19660804
  43.4 2.0 copy-start.4
  47.2 11.2 %collective-permute-start.1 = (bf16[8,128,128]{2,1,0:T(8,128)(2,1)}, bf16[8,128,128]{2,1,0:T(8,128)(2,1)S(1)}, u32[]{:S(2)}, u32[]{:S(2)}) collective-permute-start(bf16[8,128,128]{2,1,0:T(8,128)(2,1)} %cast_blocks.3), channel_id=1, source_target_pairs={{0,24},{1,25},{2,26},{3,27},{4,28},{5,29},{6,30},{7,31},{8,16},{9,... | collective-permute-start | bytes 786440 | tf_op jit(solution)/shard_map/ppermute | solution.py:499
  47.9 10.5 %collective-permute-start = (bf16[8,128,128]{2,1,0:T(8,128)(2,1)}, bf16[8,128,128]{2,1,0:T(8,128)(2,1)S(1)}, u32[]{:S(2)}, u32[]{:S(2)}) collective-permute-start(bf16[8,128,128]{2,1,0:T(8,128)(2,1)} %cast_blocks.3), channel_id=1, source_target_pairs={{0,7},{1,6},{2,5},{3,4},{4,3},{5,2},{6,1},{7,0},{8,15},{9,14},{10,... | collective-permute-start | bytes 786440 | tf_op jit(solution)/shard_map/ppermute | solution.py:500
  58.4 11.7 %copy-start.2 = (s32[8]{0:T(128)S(1)}, s32[8]{0:T(128)}, u32[]{:S(2)}) copy-start(s32[8]{0:T(128)} %bands_ref.1) | copy-start | bytes 100
  60.8 29.4 %all-to-all-start.1 = ((bf16[16,336,128]{2,1,0:T(8,128)(2,1)}), bf16[16,336,128]{2,1,0:T(8,128)(2,1)S(1)}, u32[]{:S(2)}, u32[]{:S(2)}) async-start(bf16[16,336,128]{2,1,0:T(8,128)(2,1)} %filter_rows.3), calls=%async_computation.1 | async-start | bytes 2752512 | tf_op jit(solution)/shard_map/all_to_all | solution.py:490

commit v4 on v3

--- a/solution.py
+++ b/solution.py
@@ -438,13 +438,13 @@
     levels = part.shape[2]
     columns = 4 * levels
     fifth = latitudes // 5
-    tile = [[0, 2 * fifth, 4 * fifth, latitudes], [0, fifth, 3 * fifth, latitudes]]
+    tile = [[0, latitudes // 2, latitudes], [0, fifth, latitudes]]
     smem, vmem = pl.BlockSpec(memory_space=pltpu.SMEM), pl.BlockSpec(memory_space=pltpu.VMEM)
     messages = bands.shape[0] * columns // level_cols
     grid = pltpu.VMEM((ceil_to(latitudes + depth, 8) + 8, columns), F32)
     held = 2 * (latitudes + columns) * sum(plan.widths) + 8 * (latitudes + depth) * columns
     held += 4 * messages * depth * ceil_to(level_cols, 128) + 2 * part.size
-    limit = max(52 * 1024 * 1024, held + 4 * 1024 * 1024)
+    limit = max(52 * 1024 * 1024, min(held + 8 * 1024 * 1024, 60 * 1024 * 1024))
     return pl.pallas_call(
         functools.partial(grid_kernel, plan, levels, latitudes, depth, level_cols, tile),
         out_shape=jax.ShapeDtypeStruct((messages, 2, depth, level_cols), BF),
@@ -458,7 +458,7 @@
             grid,
             grid,
             pltpu.VMEM((messages, 2, depth, level_cols), BF),
-            pltpu.SemaphoreType.DMA((2, 3)),
+            pltpu.SemaphoreType.DMA((2, 2)),
             pltpu.SemaphoreType.DMA((2, bands.shape[0])),
         ],
         compiler_params=pltpu.CompilerParams(vmem_limit_bytes=limit),

time: 254 us -> 254 us (level)
  no operation moved by 1% of the time
where the time goes in v4:
time: 254 us; the launch traced here: 253 us
  blocking collectives  149 us (59%)
  Pallas kernels  45.4 us (18%)
  waiting for transfers between devices  24.1 us (9%)
  starting transfers between devices  22.4 us (9%)
  local copies, waits for them, and re-layouts  10.7 us (4%)
    all_to_all x1, blocking collectives, per_device(): lax.all_to_all(outgoing, axes, split_axis=0, concat_axis=0, tiled=True)  149 us
    all_to_all x2, waiting for transfers between devices, exchange(): lax.all_to_all(rows, axes, split_axis=0, concat_axis=0, tiled=True, axis_...  20.3 us
    pallas_call x1, Pallas kernels, make_tables(): pl.pallas_call(functools.partial(table_kernel, plan), grid=(latitudes //...  19.7 us
    all_to_all x2, starting transfers between devices, exchange(): lax.all_to_all(rows, axes, split_axis=0, concat_axis=0, tiled=True, axis_...  13 us
    pallas_call x1, Pallas kernels, to_bands(): pl.pallas_call(functools.partial(grid_kernel, plan, levels, latitudes, de...  11 us
    unnamed x27, local copies, waits for them, and re-layouts  10.5 us
    pallas_call x2, Pallas kernels, filter_rows(): pl.pallas_call(functools.partial(filter_kernel, plan, at, levels), out_sh...  6.54 us
    ppermute x2, starting transfers between devices, swap_chunk(): far_blocks.append(lax.ppermute(own, axes, far))  5.91 us
  transfers between devices with their start and end apart: 6, of which 3 were waited for; matrix products, arithmetic and copies ran while one was open for 0% of the time, Pallas kernels for 12%

profile of v4, /device:TPU:0, one launch (start us, length us, event | category | flops | bytes accessed | tf_op | source)
XLA Modules:
  0.0 253.4 jit_solution(18428316516425314222)
XLA Ops:
  0.1 2.4 cast_blocks.2
  2.5 5.1 %collective-permute-start.3 = (bf16[32,128,128]{2,1,0:T(8,128)(2,1)}, bf16[32,128,128]{2,1,0:T(8,128)(2,1)S(1)}, u32[]{:S(2)}, u32[]{:S(2)}) collective-permute-start(bf16[32,128,128]{2,1,0:T(8,128)(2,1)} %cast_blocks.2), channel_id=1, source_target_pairs={{0,24},{1,25},{2,26},{3,27},{4,28},{5,29},{6,30},{7,31},{8,16},{9,... | collective-permute-start | bytes 3145736 | tf_op jit(solution)/shard_map/ppermute | solution.py:499
  7.6 1.6 collective-permute-start.2
  10.0 0.2 broadcast_in_dim.19.slot_ref
  10.2 4.0 %pack_rows.1 = bf16[16,336,128]{2,1,0:T(8,128)(2,1)} custom-call(s32[1]{0:T(128)} %copy.22.info_ref, s32[1280,1]{1,0:T(8,128)S(1)} %broadcast_in_dim.19.slot_ref, bf16[1281,512]{1,0:T(8,128)(2,1)S(1)} %bitcast.17), custom_call_target="tpu_custom_call" | custom-call | flops 1 | bytes 1 | tf_op jit(solution)/shard_map/pack_rows/pallas_call | solution.py:161
  14.2 3.7 %all-to-all-start = ((bf16[16,336,128]{2,1,0:T(8,128)(2,1)}), bf16[16,336,128]{2,1,0:T(8,128)(2,1)S(1)}, u32[]{:S(2)}, u32[]{:S(2)}) async-start(bf16[16,336,128]{2,1,0:T(8,128)(2,1)} %pack_rows.1), calls=%async_computation | async-start | bytes 2752512 | tf_op jit(solution)/shard_map/all_to_all | solution.py:490
  18.0 2.9 %copy-done.1 = bf16[1,1281,2560]{2,1,0:T(8,128)(2,1)S(1)} copy-done((bf16[1,1281,2560]{2,1,0:T(8,128)(2,1)S(1)}, bf16[1,1281,2560]{2,1,0:T(8,128)(2,1)}, u32[]{:S(2)}) %copy-start.1) | copy-done | bytes 6558744
  20.9 19.7 %make_tables.1 = (bf16[2560,1280]{1,0:T(8,128)(2,1)S(1)}, bf16[2560,768]{1,0:T(8,128)(2,1)S(1)}) custom-call(s32[1,1280]{1,0:T(1,128)S(1)} %broadcast_in_dim.17.upper_ref, s32[1,768]{1,0:T(1,128)S(1)} %broadcast_in_dim.18.lower_ref, bf16[1281,2560]{1,0:T(8,128)(2,1)S(1)} %bitcast.18), custom_call_target="tpu_custom_call" | custom-call | flops 134322585600 | bytes 6558720 | tf_op jit(solution)/shard_map/make_tables/pallas_call | solution.py:203
  40.6 2.8 %copy-done.3 = bf16[2560,1280]{1,0:T(8,128)(2,1)} copy-done((bf16[2560,1280]{1,0:T(8,128)(2,1)}, bf16[2560,1280]{1,0:T(8,128)(2,1)S(1)}, u32[]{:S(2)}) %copy-start.3) | copy-done | bytes 6553624
  43.4 2.0 copy-done.4
  45.4 1.8 cast_blocks.3
  47.2 0.8 collective-permute-start.1
  47.9 1.9 collective-permute-start
  49.8 0.1 pad_add_fusion.1.info_ref
  49.9 0.5 all-to-all-done.rows_ref
  50.4 4.2 %filter_rows.2 = (bf16[16,336,128]{2,1,0:T(8,128)(2,1)}, f32[64,128]{1,0:T(8,128)S(1)}) custom-call(s32[2]{0:T(128)S(1)} %pad_add_fusion.1.info_ref, bf16[16,336,128]{2,1,0:T(8,128)(2,1)S(1)} %all-to-all-done.rows_ref, bf16[32,128,128]{2,1,0:T(8,128)(2,1)} %collective-permute-done.2.near_ref, bf16[32,128,128]{2,1,0:T(8,128)(2,1)S(1)} %collective-permute-done.3.far_ref), custom_call_target="tpu_custom_call" | custom-call | flops 1073741824 | bytes 4849664 | tf_op jit(solution)/shard_map/filter_rows/pallas_call | solution.py:319
  54.6 3.8 %collective-permute-done.1.far_ref = bf16[8,128,128]{2,1,0:T(8,128)(2,1)S(1)} collective-permute-done((bf16[8,128,128]{2,1,0:T(8,128)(2,1)}, bf16[8,128,128]{2,1,0:T(8,128)(2,1)S(1)}, u32[]{:S(2)}, u32[]{:S(2)}) %collective-permute-start.1) | collective-permute-done | bytes 262176 | tf_op jit(solution)/shard_map/ppermute | solution.py:499
  58.4 2.3 filter_rows.3
  60.8 9.3 %all-to-all-start.1 = ((bf16[16,336,128]{2,1,0:T(8,128)(2,1)}), bf16[16,336,128]{2,1,0:T(8,128)(2,1)S(1)}, u32[]{:S(2)}, u32[]{:S(2)}) async-start(bf16[16,336,128]{2,1,0:T(8,128)(2,1)} %filter_rows.3), calls=%async_computation.1 | async-start | bytes 2752512 | tf_op jit(solution)/shard_map/all_to_all | solution.py:490
  70.2 0.2 reduce-window.9
  70.4 19.8 %all-to-all-done.1.part_ref = bf16[16,336,128]{2,1,0:T(8,128)(2,1)S(1)} async-done(((bf16[16,336,128]{2,1,0:T(8,128)(2,1)}), bf16[16,336,128]{2,1,0:T(8,128)(2,1)S(1)}, u32[]{:S(2)}, u32[]{:S(2)}) %all-to-all-start.1) | async-done | bytes 1376288 | tf_op jit(solution)/shard_map/all_to_all | solution.py:490
  90.2 11.0 %grid_bands.1 = bf16[32,2,400,128]{3,2,1,0:T(8,128)(2,1)} custom-call(s32[2]{0:T(128)S(1)} %pad_add_fusion.info_ref, s32[8]{0:T(128)S(1)} %bitcast_subtract_fusion.starts_ref, s32[8]{0:T(128)S(1)} %copy-done.2, bf16[16,336,128]{2,1,0:T(8,128)(2,1)S(1)} %all-to-all-done.1.part_ref, bf16[2560,1280]{1,0:T(8,128)(2,1)} %copy-done.3, bf16[2560,768]{1,0:T(8,128)(2,1)} %copy-done.4), custom_call_target="tpu_custom_call" | custom-call | flops 5368709120 | bytes 17039360 | tf_op jit(solution)/shard_map/grid_bands/pallas_call | solution.py:448
  101.2 149.4 %all_to_all.15 = bf16[64,400,128]{2,1,0:T(8,128)(2,1)S(1)} all-to-all(bf16[64,400,128]{2,1,0:T(8,128)(2,1)} %bitcast.20), channel_id=1, replica_groups=mesh['wave'=8,'lev'=4] {'wave','lev'}, dimensions={0} | all-to-all | bytes 13107200 | tf_op jit(solution)/shard_map/all_to_all | solution.py:543
  250.6 2.8 %copy.23 = bf16[64,400,128]{2,1,0:T(8,128)(2,1)} copy(bf16[64,400,128]{2,1,0:T(8,128)(2,1)S(1)} %all_to_all.15) | data formatting | bytes 13107200
  (32 shorter events, 0.2 us)
Async XLA Ops:
  0.0 9.9 %copy-start.11 = (pred[1280]{0:T(1024)(128)(4,1)S(1)}, pred[1280]{0:T(1024)(128)(4,1)}, u32[]{:S(2)}) copy-start(pred[1280]{0:T(1024)(128)(4,1)} %constant.142.clone) | copy-start | bytes 3844
  0.0 9.9 %copy-start.5 = (s32[1280]{0:T(1024)S(1)}, s32[1280]{0:T(1024)}, u32[]{:S(2)}) copy-start(s32[1280]{0:T(1024)} %constant.141.clone) | copy-start | bytes 15364
  0.0 9.9 %copy-start.6 = (s32[1280]{0:T(1024)S(1)}, s32[1280]{0:T(1024)}, u32[]{:S(2)}) copy-start(s32[1280]{0:T(1024)} %constant.140.clone) | copy-start | bytes 15364
  0.0 9.9 %copy-start.7 = (s32[1280]{0:T(1024)S(1)}, s32[1280]{0:T(1024)}, u32[]{:S(2)}) copy-start(s32[1280]{0:T(1024)} %constant.139.clone) | copy-start | bytes 15364
  0.0 9.9 %copy-start.12 = (pred[1280]{0:T(1024)(128)(4,1)S(1)}, pred[1280]{0:T(1024)(128)(4,1)}, u32[]{:S(2)}) copy-start(pred[1280]{0:T(1024)(128)(4,1)} %constant.137.clone) | copy-start | bytes 3844
  0.0 9.9 %copy-start.8 = (s32[1280]{0:T(1024)S(1)}, s32[1280]{0:T(1024)}, u32[]{:S(2)}) copy-start(s32[1280]{0:T(1024)} %constant.136.clone) | copy-start | bytes 15364
  0.0 9.9 %copy-start.9 = (s32[1280]{0:T(1024)S(1)}, s32[1280]{0:T(1024)}, u32[]{:S(2)}) copy-start(s32[1280]{0:T(1024)} %constant.135.clone) | copy-start | bytes 15364
  0.0 9.9 %copy-start.10 = (s32[1280]{0:T(1024)S(1)}, s32[1280]{0:T(1024)}, u32[]{:S(2)}) copy-start(s32[1280]{0:T(1024)} %constant.134.clone) | copy-start | bytes 15364
  0.1 10.2 %copy-start = (bf16[1,1281,512]{2,1,0:T(8,128)(2,1)S(1)}, bf16[1,1281,512]{2,1,0:T(8,128)(2,1)}, u32[]{:S(2)}) copy-start(bf16[1,1281,512]{2,1,0:T(8,128)(2,1)} %param.17) | copy-start | bytes 3935236
  2.5 47.9 %collective-permute-start.3 = (bf16[32,128,128]{2,1,0:T(8,128)(2,1)}, bf16[32,128,128]{2,1,0:T(8,128)(2,1)S(1)}, u32[]{:S(2)}, u32[]{:S(2)}) collective-permute-start(bf16[32,128,128]{2,1,0:T(8,128)(2,1)} %cast_blocks.2), channel_id=1, source_target_pairs={{0,24},{1,25},{2,26},{3,27},{4,28},{5,29},{6,30},{7,31},{8,16},{9,... | collective-permute-start | bytes 3145736 | tf_op jit(solution)/shard_map/ppermute | solution.py:499
  7.6 42.8 %collective-permute-start.2 = (bf16[32,128,128]{2,1,0:T(8,128)(2,1)}, bf16[32,128,128]{2,1,0:T(8,128)(2,1)}, u32[]{:S(2)}, u32[]{:S(2)}) collective-permute-start(bf16[32,128,128]{2,1,0:T(8,128)(2,1)} %cast_blocks.2), channel_id=1, source_target_pairs={{0,7},{1,6},{2,5},{3,4},{4,3},{5,2},{6,1},{7,0},{8,15},{9,14},{10,... | collective-permute-start | bytes 3145736 | tf_op jit(solution)/shard_map/ppermute | solution.py:500
  14.2 36.2 %all-to-all-start = ((bf16[16,336,128]{2,1,0:T(8,128)(2,1)}), bf16[16,336,128]{2,1,0:T(8,128)(2,1)S(1)}, u32[]{:S(2)}, u32[]{:S(2)}) async-start(bf16[16,336,128]{2,1,0:T(8,128)(2,1)} %pack_rows.1), calls=%async_computation | async-start | bytes 2752512 | tf_op jit(solution)/shard_map/all_to_all | solution.py:490
  18.0 2.9 %copy-start.1 = (bf16[1,1281,2560]{2,1,0:T(8,128)(2,1)S(1)}, bf16[1,1281,2560]{2,1,0:T(8,128)(2,1)}, u32[]{:S(2)}) copy-start(bf16[1,1281,2560]{2,1,0:T(8,128)(2,1)} %param.19) | copy-start | bytes 19676164
  40.6 2.8 %copy-start.3 = (bf16[2560,1280]{1,0:T(8,128)(2,1)}, bf16[2560,1280]{1,0:T(8,128)(2,1)S(1)}, u32[]{:S(2)}) copy-start(bf16[2560,1280]{1,0:T(8,128)(2,1)S(1)} %get-tuple-element.31.refs_0_) | copy-start | bytes 19660804
  43.4 2.0 copy-start.4
  47.2 11.2 %collective-permute-start.1 = (bf16[8,128,128]{2,1,0:T(8,128)(2,1)}, bf16[8,128,128]{2,1,0:T(8,128)(2,1)S(1)}, u32[]{:S(2)}, u32[]{:S(2)}) collective-permute-start(bf16[8,128,128]{2,1,0:T(8,128)(2,1)} %cast_blocks.3), channel_id=1, source_target_pairs={{0,24},{1,25},{2,26},{3,27},{4,28},{5,29},{6,30},{7,31},{8,16},{9,... | collective-permute-start | bytes 786440 | tf_op jit(solution)/shard_map/ppermute | solution.py:499
  47.9 10.5 %collective-permute-start = (bf16[8,128,128]{2,1,0:T(8,128)(2,1)}, bf16[8,128,128]{2,1,0:T(8,128)(2,1)S(1)}, u32[]{:S(2)}, u32[]{:S(2)}) collective-permute-start(bf16[8,128,128]{2,1,0:T(8,128)(2,1)} %cast_blocks.3), channel_id=1, source_target_pairs={{0,7},{1,6},{2,5},{3,4},{4,3},{5,2},{6,1},{7,0},{8,15},{9,14},{10,... | collective-permute-start | bytes 786440 | tf_op jit(solution)/shard_map/ppermute | solution.py:500
  58.4 11.7 %copy-start.2 = (s32[8]{0:T(128)S(1)}, s32[8]{0:T(128)}, u32[]{:S(2)}) copy-start(s32[8]{0:T(128)} %bands_ref.1) | copy-start | bytes 100
  60.8 29.4 %all-to-all-start.1 = ((bf16[16,336,128]{2,1,0:T(8,128)(2,1)}), bf16[16,336,128]{2,1,0:T(8,128)(2,1)S(1)}, u32[]{:S(2)}, u32[]{:S(2)}) async-start(bf16[16,336,128]{2,1,0:T(8,128)(2,1)} %filter_rows.3), calls=%async_computation.1 | async-start | bytes 2752512 | tf_op jit(solution)/shard_map/all_to_all | solution.py:490

commit v5 on v2

--- a/solution.py
+++ b/solution.py
@@ -232,10 +232,18 @@
     first_fold = (info_ref[1] + fold0).astype(F32)
     swap = swap_matrix()
 
-    near = pltpu.make_async_copy(near_ref, held_ref.at[info_ref[0]], in_sems.at[0])
-    far = pltpu.make_async_copy(far_ref, held_ref.at[1 - info_ref[0]], in_sems.at[1])
-    near.start()
-    far.start()
+    arrivals = []
+    if first:
+        for side, (ref, place) in enumerate(((near_ref, info_ref[0]), (far_ref, 1 - info_ref[0]))):
+            arrivals.append(pltpu.make_async_copy(ref, held_ref.at[place], in_sems.at[side]))
+            arrivals[side].start()
+
+    def matrices(i):
+        at = count - 1 - i
+        if first:
+            return [held_ref[0, i], held_ref[1, at]]
+        is_high = info_ref[0] == 1
+        return [jnp.where(is_high, far_ref[i], near_ref[i]), jnp.where(is_high, near_ref[at], far_ref[at])]
 
     def turn(rows):
         return jnp.dot(swap, rows, preferred_element_type=F32)
@@ -257,8 +265,8 @@
         else:
             kept = before_ref[4 * SUB * g:4 * SUB * (g + 1), :]
         tails.append((tail[:4 * SUB].astype(BF), jnp.concatenate([low] * 4, axis=0), kept))
-    near.wait()
-    far.wait()
+    for arrival in arrivals:
+        arrival.wait()
 
     for g in range(groups):
         sources = slice(g * SUB, (g + 1) * SUB)
@@ -269,8 +277,9 @@
                 return [x_ref[start:start + SUB, c * levels:(c + 1) * levels] for c in range(4)]
 
             rows = jnp.concatenate([*stack(i), *stack(count + i), extra], axis=0)
-            matrices = jnp.concatenate([held_ref[0, i], held_ref[1, count - 1 - i]], axis=0)
-            both = lax.dot_general(rows, matrices, (((1,), (1,)), ((), ())), preferred_element_type=F32)
+            both = lax.dot_general(
+                rows, jnp.concatenate(matrices(i), axis=0), (((1,), (1,)), ((), ())), preferred_element_type=F32
+            )
             from_low, from_high = both[:4 * SUB, :levels], both[:, levels:]
             fold = first_fold + i
             mixed = jnp.where(low <= fold, from_low, from_high[:4 * SUB])
@@ -319,7 +328,7 @@
     return pl.pallas_call(
         functools.partial(filter_kernel, plan, at, levels),
         out_shape=out_shape,
-        in_specs=[smem, vmem, anywhere, anywhere] + ([vmem, anywhere] if before else []),
+        in_specs=[smem, vmem] + ([vmem, vmem, vmem, anywhere] if before else [anywhere, anywhere]),
         out_specs=[anywhere] + [vmem] * (len(out_shape) - 1),
         input_output_aliases={5: 0} if before else {},
         scratch_shapes=[
@@ -388,26 +397,30 @@
         return pltpu.make_async_copy(cut_ref.at[messages, half], out_ref.at[messages, half], out_sems.at[half, w])
 
     def cut(half, w):
-        place = lax.broadcasted_iota(jnp.int32, (8, 4 * levels), 0)
+        place = lax.broadcasted_iota(jnp.int32, (8, levels), 0)
         start = starts_ref[w]
         base = start // 8 * 8
         offset = start - base
+        front = place < 8 - offset
 
         def slab(at):
-            held = grids[half][pl.ds(pl.multiple_of(base + at, 8), 8), :]
-            return pltpu.roll(held, (8 - offset) % 8, axis=0)
+            rows = pl.ds(pl.multiple_of(base + at, 8), 8)
+            held = [grids[half][rows, c * levels:(c + 1) * levels] for c in range(4)]
+            return [pltpu.roll(part, (8 - offset) % 8, axis=0) for part in held]
 
         after = slab(0)
         done = []
         for r in range(0, depth, 8):
             now, after = after, slab(r + 8)
-            got = jnp.where(place < 8 - offset, now, after)
-            done.append(jnp.where(place < bands_ref[w] - r, got, 0.0))
+            inside = place < bands_ref[w] - r
+            done.append([jnp.where(inside, jnp.where(front, *pair), 0.0) for pair in zip(now, after)])
             if len(done) == 2 or r + 8 == depth:
-                rows = jnp.concatenate(done, axis=0).astype(BF)
-                first = r + 8 - rows.shape[0]
-                for g in range(groups):
-                    cut_ref[w * groups + g, half, first:r + 8, :] = rows[:, g * level_cols:(g + 1) * level_cols]
+                first = r + 8 - 8 * len(done)
+                for c, parts in enumerate(zip(*done)):
+                    rows = jnp.concatenate(parts, axis=0).astype(BF)
+                    for at in range(0, levels, level_cols):
+                        message = w * groups + (c * levels + at) // level_cols
+                        cut_ref[message, half, first:r + 8, :] = rows[:, at:at + level_cols]
                 done = []
         departure(half, w).start()
 

time: 254 us -> 253 us (level)
  no operation moved by 1% of the time
where the time goes in v5:
time: 253 us
  blocking collectives  149 us (59%)
  Pallas kernels  45 us (18%)
  waiting for transfers between devices  24.1 us (10%)
  starting transfers between devices  22.4 us (9%)
  local copies, waits for them, and re-layouts  10.7 us (4%)
    all_to_all x1, blocking collectives, per_device(): lax.all_to_all(outgoing, axes, split_axis=0, concat_axis=0, tiled=True)  149 us
    all_to_all x2, waiting for transfers between devices, exchange(): lax.all_to_all(rows, axes, split_axis=0, concat_axis=0, tiled=True, axis_...  20.3 us
    pallas_call x1, Pallas kernels, make_tables(): pl.pallas_call(functools.partial(table_kernel, plan), grid=(latitudes //...  19.7 us
    all_to_all x2, starting transfers between devices, exchange(): lax.all_to_all(rows, axes, split_axis=0, concat_axis=0, tiled=True, axis_...  13 us
    pallas_call x1, Pallas kernels, to_bands(): pl.pallas_call(functools.partial(grid_kernel, plan, levels, latitudes, de...  10.8 us
    unnamed x27, local copies, waits for them, and re-layouts  10.5 us
    pallas_call x2, Pallas kernels, filter_rows(): pl.pallas_call(functools.partial(filter_kernel, plan, at, levels), out_sh...  6.34 us
    ppermute x2, starting transfers between devices, swap_chunk(): far_blocks.append(lax.ppermute(own, axes, far))  5.92 us
  transfers between devices with their start and end apart: 6, of which 3 were waited for; matrix products, arithmetic and copies ran while one was open for 0% of the time, Pallas kernels for 12%

profile of v5, /device:TPU:0, one launch (start us, length us, event | category | flops | bytes accessed | tf_op | source)
XLA Modules:
  0.0 253.0 jit_solution(13490978790103365398)
XLA Ops:
  0.1 2.4 cast_blocks.2
  2.5 5.1 %collective-permute-start.3 = (bf16[32,128,128]{2,1,0:T(8,128)(2,1)}, bf16[32,128,128]{2,1,0:T(8,128)(2,1)S(1)}, u32[]{:S(2)}, u32[]{:S(2)}) collective-permute-start(bf16[32,128,128]{2,1,0:T(8,128)(2,1)} %cast_blocks.2), channel_id=1, source_target_pairs={{0,24},{1,25},{2,26},{3,27},{4,28},{5,29},{6,30},{7,31},{8,16},{9,... | collective-permute-start | bytes 3145736 | tf_op jit(solution)/shard_map/ppermute | solution.py:502
  7.6 1.6 collective-permute-start.2
  10.0 0.2 broadcast_in_dim.19.slot_ref
  10.2 4.0 %pack_rows.1 = bf16[16,336,128]{2,1,0:T(8,128)(2,1)} custom-call(s32[1]{0:T(128)} %copy.22.info_ref, s32[1280,1]{1,0:T(8,128)S(1)} %broadcast_in_dim.19.slot_ref, bf16[1281,512]{1,0:T(8,128)(2,1)S(1)} %bitcast.17), custom_call_target="tpu_custom_call" | custom-call | flops 1 | bytes 1 | tf_op jit(solution)/shard_map/pack_rows/pallas_call | solution.py:161
  14.2 3.7 %all-to-all-start = ((bf16[16,336,128]{2,1,0:T(8,128)(2,1)}), bf16[16,336,128]{2,1,0:T(8,128)(2,1)S(1)}, u32[]{:S(2)}, u32[]{:S(2)}) async-start(bf16[16,336,128]{2,1,0:T(8,128)(2,1)} %pack_rows.1), calls=%async_computation | async-start | bytes 2752512 | tf_op jit(solution)/shard_map/all_to_all | solution.py:493
  18.0 2.9 %copy-done.1 = bf16[1,1281,2560]{2,1,0:T(8,128)(2,1)S(1)} copy-done((bf16[1,1281,2560]{2,1,0:T(8,128)(2,1)S(1)}, bf16[1,1281,2560]{2,1,0:T(8,128)(2,1)}, u32[]{:S(2)}) %copy-start.1) | copy-done | bytes 6558744
  20.9 19.7 %make_tables.1 = (bf16[2560,1280]{1,0:T(8,128)(2,1)S(1)}, bf16[2560,768]{1,0:T(8,128)(2,1)S(1)}) custom-call(s32[1,1280]{1,0:T(1,128)S(1)} %broadcast_in_dim.17.upper_ref, s32[1,768]{1,0:T(1,128)S(1)} %broadcast_in_dim.18.lower_ref, bf16[1281,2560]{1,0:T(8,128)(2,1)S(1)} %bitcast.18), custom_call_target="tpu_custom_call" | custom-call | flops 134322585600 | bytes 6558720 | tf_op jit(solution)/shard_map/make_tables/pallas_call | solution.py:203
  40.6 2.8 %copy-done.3 = bf16[2560,1280]{1,0:T(8,128)(2,1)} copy-done((bf16[2560,1280]{1,0:T(8,128)(2,1)}, bf16[2560,1280]{1,0:T(8,128)(2,1)S(1)}, u32[]{:S(2)}) %copy-start.3) | copy-done | bytes 6553624
  43.4 2.0 copy-done.4
  45.4 1.8 cast_blocks.3
  47.1 0.8 collective-permute-start.1
  47.9 1.9 collective-permute-start
  49.8 0.1 pad_add_fusion.1.info_ref
  49.9 0.5 all-to-all-done.rows_ref
  50.4 4.2 %filter_rows.2 = (bf16[16,336,128]{2,1,0:T(8,128)(2,1)}, f32[64,128]{1,0:T(8,128)S(1)}) custom-call(s32[2]{0:T(128)S(1)} %pad_add_fusion.1.info_ref, bf16[16,336,128]{2,1,0:T(8,128)(2,1)S(1)} %all-to-all-done.rows_ref, bf16[32,128,128]{2,1,0:T(8,128)(2,1)} %collective-permute-done.2.near_ref, bf16[32,128,128]{2,1,0:T(8,128)(2,1)S(1)} %collective-permute-done.3.far_ref), custom_call_target="tpu_custom_call" | custom-call | flops 1073741824 | bytes 4849664 | tf_op jit(solution)/shard_map/filter_rows/pallas_call | solution.py:328
  54.6 3.8 %collective-permute-done.1.far_ref = bf16[8,128,128]{2,1,0:T(8,128)(2,1)S(1)} collective-permute-done((bf16[8,128,128]{2,1,0:T(8,128)(2,1)}, bf16[8,128,128]{2,1,0:T(8,128)(2,1)S(1)}, u32[]{:S(2)}, u32[]{:S(2)}) %collective-permute-start.1) | collective-permute-done | bytes 262176 | tf_op jit(solution)/shard_map/ppermute | solution.py:502
  58.4 2.2 filter_rows.3
  60.6 9.3 %all-to-all-start.1 = ((bf16[16,336,128]{2,1,0:T(8,128)(2,1)}), bf16[16,336,128]{2,1,0:T(8,128)(2,1)S(1)}, u32[]{:S(2)}, u32[]{:S(2)}) async-start(bf16[16,336,128]{2,1,0:T(8,128)(2,1)} %filter_rows.3), calls=%async_computation.1 | async-start | bytes 2752512 | tf_op jit(solution)/shard_map/all_to_all | solution.py:493
  70.0 0.2 reduce-window.9
  70.2 19.8 %all-to-all-done.1.part_ref = bf16[16,336,128]{2,1,0:T(8,128)(2,1)S(1)} async-done(((bf16[16,336,128]{2,1,0:T(8,128)(2,1)}), bf16[16,336,128]{2,1,0:T(8,128)(2,1)S(1)}, u32[]{:S(2)}, u32[]{:S(2)}) %all-to-all-start.1) | async-done | bytes 1376288 | tf_op jit(solution)/shard_map/all_to_all | solution.py:493
  90.0 10.8 %grid_bands.1 = bf16[32,2,400,128]{3,2,1,0:T(8,128)(2,1)} custom-call(s32[2]{0:T(128)S(1)} %pad_add_fusion.info_ref, s32[8]{0:T(128)S(1)} %bitcast_subtract_fusion.starts_ref, s32[8]{0:T(128)S(1)} %copy-done.2, bf16[16,336,128]{2,1,0:T(8,128)(2,1)S(1)} %all-to-all-done.1.part_ref, bf16[2560,1280]{1,0:T(8,128)(2,1)} %copy-done.3, bf16[2560,768]{1,0:T(8,128)(2,1)} %copy-done.4), custom_call_target="tpu_custom_call" | custom-call | flops 5368709120 | bytes 17039360 | tf_op jit(solution)/shard_map/grid_bands/pallas_call | solution.py:451
  100.8 149.4 %all_to_all.15 = bf16[64,400,128]{2,1,0:T(8,128)(2,1)S(1)} all-to-all(bf16[64,400,128]{2,1,0:T(8,128)(2,1)} %bitcast.20), channel_id=1, replica_groups=mesh['wave'=8,'lev'=4] {'wave','lev'}, dimensions={0} | all-to-all | bytes 13107200 | tf_op jit(solution)/shard_map/all_to_all | solution.py:546
  250.2 2.8 %copy.23 = bf16[64,400,128]{2,1,0:T(8,128)(2,1)} copy(bf16[64,400,128]{2,1,0:T(8,128)(2,1)S(1)} %all_to_all.15) | data formatting | bytes 13107200
  (32 shorter events, 0.2 us)
Async XLA Ops:
  0.0 9.9 %copy-start.11 = (pred[1280]{0:T(1024)(128)(4,1)S(1)}, pred[1280]{0:T(1024)(128)(4,1)}, u32[]{:S(2)}) copy-start(pred[1280]{0:T(1024)(128)(4,1)} %constant.142.clone) | copy-start | bytes 3844
  0.0 9.9 %copy-start.5 = (s32[1280]{0:T(1024)S(1)}, s32[1280]{0:T(1024)}, u32[]{:S(2)}) copy-start(s32[1280]{0:T(1024)} %constant.141.clone) | copy-start | bytes 15364
  0.0 9.9 %copy-start.6 = (s32[1280]{0:T(1024)S(1)}, s32[1280]{0:T(1024)}, u32[]{:S(2)}) copy-start(s32[1280]{0:T(1024)} %constant.140.clone) | copy-start | bytes 15364
  0.0 9.9 %copy-start.7 = (s32[1280]{0:T(1024)S(1)}, s32[1280]{0:T(1024)}, u32[]{:S(2)}) copy-start(s32[1280]{0:T(1024)} %constant.139.clone) | copy-start | bytes 15364
  0.0 9.9 %copy-start.12 = (pred[1280]{0:T(1024)(128)(4,1)S(1)}, pred[1280]{0:T(1024)(128)(4,1)}, u32[]{:S(2)}) copy-start(pred[1280]{0:T(1024)(128)(4,1)} %constant.137.clone) | copy-start | bytes 3844
  0.0 9.9 %copy-start.8 = (s32[1280]{0:T(1024)S(1)}, s32[1280]{0:T(1024)}, u32[]{:S(2)}) copy-start(s32[1280]{0:T(1024)} %constant.136.clone) | copy-start | bytes 15364
  0.0 9.9 %copy-start.9 = (s32[1280]{0:T(1024)S(1)}, s32[1280]{0:T(1024)}, u32[]{:S(2)}) copy-start(s32[1280]{0:T(1024)} %constant.135.clone) | copy-start | bytes 15364
  0.0 9.9 %copy-start.10 = (s32[1280]{0:T(1024)S(1)}, s32[1280]{0:T(1024)}, u32[]{:S(2)}) copy-start(s32[1280]{0:T(1024)} %constant.134.clone) | copy-start | bytes 15364
  0.1 10.2 %copy-start = (bf16[1,1281,512]{2,1,0:T(8,128)(2,1)S(1)}, bf16[1,1281,512]{2,1,0:T(8,128)(2,1)}, u32[]{:S(2)}) copy-start(bf16[1,1281,512]{2,1,0:T(8,128)(2,1)} %param.17) | copy-start | bytes 3935236
  2.5 47.9 %collective-permute-start.3 = (bf16[32,128,128]{2,1,0:T(8,128)(2,1)}, bf16[32,128,128]{2,1,0:T(8,128)(2,1)S(1)}, u32[]{:S(2)}, u32[]{:S(2)}) collective-permute-start(bf16[32,128,128]{2,1,0:T(8,128)(2,1)} %cast_blocks.2), channel_id=1, source_target_pairs={{0,24},{1,25},{2,26},{3,27},{4,28},{5,29},{6,30},{7,31},{8,16},{9,... | collective-permute-start | bytes 3145736 | tf_op jit(solution)/shard_map/ppermute | solution.py:502
  7.6 42.8 %collective-permute-start.2 = (bf16[32,128,128]{2,1,0:T(8,128)(2,1)}, bf16[32,128,128]{2,1,0:T(8,128)(2,1)}, u32[]{:S(2)}, u32[]{:S(2)}) collective-permute-start(bf16[32,128,128]{2,1,0:T(8,128)(2,1)} %cast_blocks.2), channel_id=1, source_target_pairs={{0,7},{1,6},{2,5},{3,4},{4,3},{5,2},{6,1},{7,0},{8,15},{9,14},{10,... | collective-permute-start | bytes 3145736 | tf_op jit(solution)/shard_map/ppermute | solution.py:503
  14.2 36.2 %all-to-all-start = ((bf16[16,336,128]{2,1,0:T(8,128)(2,1)}), bf16[16,336,128]{2,1,0:T(8,128)(2,1)S(1)}, u32[]{:S(2)}, u32[]{:S(2)}) async-start(bf16[16,336,128]{2,1,0:T(8,128)(2,1)} %pack_rows.1), calls=%async_computation | async-start | bytes 2752512 | tf_op jit(solution)/shard_map/all_to_all | solution.py:493
  18.0 2.9 %copy-start.1 = (bf16[1,1281,2560]{2,1,0:T(8,128)(2,1)S(1)}, bf16[1,1281,2560]{2,1,0:T(8,128)(2,1)}, u32[]{:S(2)}) copy-start(bf16[1,1281,2560]{2,1,0:T(8,128)(2,1)} %param.19) | copy-start | bytes 19676164
  40.6 2.8 %copy-start.3 = (bf16[2560,1280]{1,0:T(8,128)(2,1)}, bf16[2560,1280]{1,0:T(8,128)(2,1)S(1)}, u32[]{:S(2)}) copy-start(bf16[2560,1280]{1,0:T(8,128)(2,1)S(1)} %get-tuple-element.31.refs_0_) | copy-start | bytes 19660804
  43.4 2.0 copy-start.4
  47.1 11.3 %collective-permute-start.1 = (bf16[8,128,128]{2,1,0:T(8,128)(2,1)}, bf16[8,128,128]{2,1,0:T(8,128)(2,1)S(1)}, u32[]{:S(2)}, u32[]{:S(2)}) collective-permute-start(bf16[8,128,128]{2,1,0:T(8,128)(2,1)} %cast_blocks.3), channel_id=1, source_target_pairs={{0,24},{1,25},{2,26},{3,27},{4,28},{5,29},{6,30},{7,31},{8,16},{9,... | collective-permute-start | bytes 786440 | tf_op jit(solution)/shard_map/ppermute | solution.py:502
  47.9 10.5 %collective-permute-start = (bf16[8,128,128]{2,1,0:T(8,128)(2,1)}, bf16[8,128,128]{2,1,0:T(8,128)(2,1)S(1)}, u32[]{:S(2)}, u32[]{:S(2)}) collective-permute-start(bf16[8,128,128]{2,1,0:T(8,128)(2,1)} %cast_blocks.3), channel_id=1, source_target_pairs={{0,7},{1,6},{2,5},{3,4},{4,3},{5,2},{6,1},{7,0},{8,15},{9,14},{10,... | collective-permute-start | bytes 786440 | tf_op jit(solution)/shard_map/ppermute | solution.py:503
  58.4 11.5 %copy-start.2 = (s32[8]{0:T(128)S(1)}, s32[8]{0:T(128)}, u32[]{:S(2)}) copy-start(s32[8]{0:T(128)} %bands_ref.1) | copy-start | bytes 100
  60.6 29.4 %all-to-all-start.1 = ((bf16[16,336,128]{2,1,0:T(8,128)(2,1)}), bf16[16,336,128]{2,1,0:T(8,128)(2,1)S(1)}, u32[]{:S(2)}, u32[]{:S(2)}) async-start(bf16[16,336,128]{2,1,0:T(8,128)(2,1)} %filter_rows.3), calls=%async_computation.1 | async-start | bytes 2752512 | tf_op jit(solution)/shard_map/all_to_all | solution.py:493
